TPU v7x, 512 devices: a whole 4x4x16 slice. The times are simulated.
512 devices in a mesh: grp: 16 (over z), ctx: 32 (over x, y, core).
Axes of the slice: x: 4, y: 4, z: 16, core: 2. Of those that a mesh axis runs over, the one named last changes fastest.
Arguments:
- query: bfloat16 [2048, 128, 192], P('grp', 'ctx'), may hold values from -44 to 44
- absorb_k: bfloat16 [128, 128, 512], P('ctx'), may hold values from -0.5 to 0.5
- absorb_v: bfloat16 [128, 512, 128], P('ctx'), may hold values from -0.25 to 0.25
- latent_cache: bfloat16 [32768, 576], P('ctx'), may hold values from -6 to 6
- cold_blocks: int32 [2048, 30], P(('grp', 'ctx')), may hold values from 0 to 509, as said below
Outputs:
- attended: bfloat16 [2048, 128, 128], P('grp', 'ctx')
Inputs may be any that keep to these rules, and one draw needn't show every extreme that they name: `cold_blocks`: each row names 30 distinct blocks, none of the newest 2. Over the 4 rows of one device (aligned groups of rows in order), at most 2 distinct named blocks lie in the 16 blocks of any one ctx index; the share of the last ctx index reaches 2 in every such group.
All inputs are finite; a program needn't handle non-finite values.
Results may differ from a plain program's by a relative error of at most 0.0067.
Values may be sent and summed in bfloat16 or wider, within the bound.
A program may use at most 64 MiB of HBM per device.

v0:
```python
import math

import jax
import jax.numpy as jnp
from jax import lax
from jax.sharding import PartitionSpec as P

DL = 512
DN = 128
BLK = 64
TOPB = 32
HOT = 2


def fetch_blocks(latent_cache, requests):
    width = latent_cache.shape[1]
    per_owner = latent_cache.shape[0] // BLK
    stored = latent_cache.reshape(per_owner, BLK, width)
    blocks = jnp.take(
        stored, lax.all_to_all(requests, "ctx", split_axis=0, concat_axis=0, tiled=True), axis=0
    )
    return lax.all_to_all(blocks, "ctx", split_axis=0, concat_axis=0, tiled=True)


def body(query, absorb_k, absorb_v, latent_cache, cold_blocks):
    owners = lax.axis_size("ctx")
    width = latent_cache.shape[1]
    per_owner = latent_cache.shape[0] // BLK
    total_blocks = per_owner * owners
    cold_cap = max(2, 2 * (TOPB - HOT) // owners)
    scale = 1.0 / math.sqrt(query.shape[-1])
    q_lat = jnp.einsum(
        "rhn,hnl->rhl", query[:, :, :DN], absorb_k, preferred_element_type=jnp.float32
    )
    q_full = jnp.concatenate([q_lat, query[:, :, DN:].astype(jnp.float32)], axis=-1).astype(
        jnp.bfloat16
    )
    local_q = lax.all_to_all(q_full, "ctx", split_axis=0, concat_axis=1, tiled=True)
    rows = local_q.shape[0]
    block_range = jnp.arange(total_blocks, dtype=jnp.int32)
    newest = total_blocks - HOT + jnp.arange(HOT, dtype=jnp.int32)
    flat_picks = cold_blocks.reshape(-1)
    needed = jnp.any(flat_picks[:, None] == block_range[None, :], axis=0)
    needed = needed | (block_range >= total_blocks - HOT)
    capacity = HOT + cold_cap
    needed = needed.reshape(owners, per_owner)
    counted = needed.astype(jnp.int32)
    rank = jnp.cumsum(counted, axis=1) - counted
    slot_range = jnp.arange(capacity, dtype=jnp.int32)
    selected = needed[:, :, None] & (rank[:, :, None] == slot_range[None, None, :])
    local_ids = jnp.arange(per_owner, dtype=jnp.int32)[None, :, None]
    requests = jnp.sum(jnp.where(selected, local_ids, 0), axis=1)
    fetched = fetch_blocks(latent_cache, requests).reshape(owners * capacity, BLK, width)
    table = (jnp.arange(owners, dtype=jnp.int32)[:, None] * capacity + rank).reshape(-1)
    all_picks = jnp.concatenate(
        [jnp.broadcast_to(newest[None, :], (rows, HOT)), cold_blocks], axis=1
    )
    match = all_picks[..., None] == block_range
    positions = jnp.sum(jnp.where(match, table, 0), axis=-1)

    def attend_block(items):
        q_block, pos_block = items
        keys = jnp.take(fetched, pos_block, axis=0).reshape(q_block.shape[0], -1, width)
        scores = (
            jnp.einsum("rhc,rkc->rhk", q_block, keys, preferred_element_type=jnp.float32) * scale
        )
        highest = jnp.max(scores, axis=-1, keepdims=True)
        weights = jnp.exp(scores - highest)
        probs = (weights / jnp.sum(weights, axis=-1, keepdims=True)).astype(jnp.bfloat16)
        return jnp.einsum(
            "rhk,rkl->rhl", probs, keys[:, :, :DL], preferred_element_type=jnp.float32
        ).astype(jnp.bfloat16)

    heads = local_q.shape[1]
    q_blocks = local_q.reshape(rows // 4, 4, heads, width)
    pos_blocks = positions.reshape(rows // 4, 4, positions.shape[1])
    out_lat = lax.map(attend_block, (q_blocks, pos_blocks)).reshape(rows, heads, DL)
    returned = lax.all_to_all(out_lat, "ctx", split_axis=1, concat_axis=0, tiled=True)
    attended = jnp.einsum("rhl,hlv->rhv", returned, absorb_v, preferred_element_type=jnp.float32)
    return attended.astype(jnp.bfloat16)


def solution(mesh):
    placed = (
        P("grp", "ctx", None),
        P("ctx", None, None),
        P("ctx", None, None),
        P("ctx", None),
        P(("grp", "ctx"), None),
    )
    return jax.shard_map(
        body, mesh=mesh, in_specs=placed, out_specs=P("grp", "ctx", None), check_vma=False
    )
```

profile of v0, /device:TPU:1, one launch (start us, length us, event | category | flops | bytes accessed | tf_op | source)
XLA Modules:
  0.0 267.5 jit_solution(9872641858246843702)
XLA Ops:
  0.0 0.0 copy-start
  0.0 0.8 eq.44
  0.8 0.1 fusion.13
  0.9 0.1 reduce_or.12
  1.1 0.2 reduce_window_sum.13
  1.2 0.1 copy.45
  1.3 0.1 copy.44
  1.4 0.7 copy.46
  2.1 10.4 %all-to-all-start.1 = ((s32[32,1,4]{2,1,0:T(1,128)}), s32[32,1,4]{2,1,0:T(1,128)S(1)}, u32[]{:S(2)}, u32[]{:S(2)}) async-start(s32[32,1,4]{2,1,0:T(1,128)} %copy.46), calls=%async_computation.1 | async-start | bytes 32768 | tf_op jit(solution)/shard_map/all_to_all | solution.py:20
  12.5 0.9 slice.11
  13.3 0.0 copy-done
  13.4 1.3 fusion.9
  14.7 1.7 copy.49
  16.3 1.4 copy.42
  17.7 1.8 all-to-all-done.1
  19.5 5.7 %all-to-all-start = ((bf16[128,4,576]{2,1,0:T(4,128)(2,1)}), bf16[128,4,576]{2,1,0:T(4,128)(2,1)S(1)}, u32[]{:S(2)}, u32[]{:S(2)}) async-start(bf16[128,4,576]{2,1,0:T(4,128)(2,1)} %copy.42), calls=%async_computation | async-start | bytes 1310720 | tf_op jit(solution)/shard_map/all_to_all | solution.py:38
  25.2 0.1 copy.47
  25.3 0.1 copy.51
  25.4 0.1 reshape.118
  25.5 0.1 copy.48
  25.6 7.4 %gather_fusion = bf16[128,64,576]{2,1,0:T(8,128)(2,1)} fusion(bf16[16,64,576]{2,1,0:T(8,128)(2,1)S(1)} %bitcast.37, s32[1024]{0:T(1024)S(1)} %pad_clamp_fusion.1), kind=kCustom, calls=%fused_computation | custom fusion | bytes 18874880 | tf_op jit(solution)/shard_map/jit(_take)/gather | solution.py:19
  33.0 10.1 %broadcast_select_fusion = bf16[32,4,64,576]{3,2,1,0:T(8,128)(2,1)} fusion(bf16[32,4,64,576]{3,2,1,0:T(8,128)(2,1)} %bitcast.39, pred[32,4]{1,0:T(8,128)(4,1)S(1)} %copy.48), kind=kLoop, calls=%fused_computation.4 | loop fusion | flops 4718592 | bytes 18874496 | tf_op jit(solution)/shard_map/jit(_take)/select_n | solution.py:19
  43.2 0.0 copy-start.4
  43.2 0.0 all-to-all-done
  43.2 7.6 %all-to-all-start.2 = ((bf16[32,4,64,576]{3,2,1,0:T(8,128)(2,1)}), bf16[32,4,64,576]{3,2,1,0:T(8,128)(2,1)}, u32[]{:S(2)}, u32[]{:S(2)}) async-start(bf16[32,4,64,576]{3,2,1,0:T(8,128)(2,1)} %broadcast_select_fusion), calls=%async_computation.2 | async-start | bytes 20971520 | tf_op jit(solution)/shard_map/all_to_all | solution.py:22
  50.7 0.1 reduce_window_sum.14
  50.8 0.1 add.73
  50.9 0.1 add.74
  51.0 0.0 copy-done.4
  51.0 0.1 pad_add_fusion
  51.1 0.2 select_reduce_fusion
  51.3 0.1 broadcast_in_dim.71
  51.4 0.1 broadcast_in_dim.72
  51.5 0.1 reshape.126
  51.6 0.3 copy.43
  51.9 139.9 %all-to-all-done.2 = bf16[32,4,64,576]{3,2,1,0:T(8,128)(2,1)} async-done(((bf16[32,4,64,576]{3,2,1,0:T(8,128)(2,1)}), bf16[32,4,64,576]{3,2,1,0:T(8,128)(2,1)}, u32[]{:S(2)}, u32[]{:S(2)}) %all-to-all-start.2) | async-done | bytes 9437216 | tf_op jit(solution)/shard_map/all_to_all | solution.py:22
  191.8 11.8 %gather_fusion.1 = bf16[128,64,576]{2,1,0:T(8,128)(2,1)} fusion(bf16[128,64,576]{2,1,0:T(8,128)(2,1)} %bitcast.9, s32[1024]{0:T(1024)S(1)} %pad_clamp_fusion), kind=kCustom, calls=%fused_computation.1 | custom fusion | bytes 18874880 | tf_op jit(solution)/shard_map/while/body/eval_jaxpr/jit(_take)/gather | solution.py:63
  203.6 6.4 %bitcast_select_fusion = bf16[4,2048,576]{2,1,0:T(8,128)(2,1)S(1)} fusion(pred[4,2048]{1,0:T(4,128)(4,1)S(1)} %broadcast_in_dim.72, bf16[4,2048,576]{2,1,0:T(8,128)(2,1)} %bitcast.38), kind=kLoop, calls=%fused_computation.3 | loop fusion | flops 4718592 | bytes 18882560 | tf_op jit(solution)/shard_map/while/body/eval_jaxpr/jit(_take)/select_n | solution.py:63
  210.1 0.0 copy-start.1
  210.1 3.5 %fusion.11 = f32[4,128,2048]{2,1,0:T(8,128)S(1)} fusion(bf16[4,2048,576]{2,1,0:T(8,128)(2,1)S(1)} %bitcast_select_fusion, bf16[4,128,576]{2,0,1:T(4,128)(2,1)S(1)} %bitcast.40), kind=kOutput, calls=%fused_computation.18 | convolution fusion | flops 1207959552 | bytes 14221312 | tf_op jit(solution)/shard_map/while/body/eval_jaxpr/rhc,rkc->rhk/dot_general | solution.py:65
  213.6 0.5 copy-done.1
  214.0 0.0 copy-start.2
  214.0 2.1 copy-done.2
  216.1 1.3 fusion.27
  217.4 6.5 %fusion.6 = bf16[4,128,512]{2,1,0:T(8,128)(2,1)S(1)} fusion(bf16[4,2048,576]{2,1,0:T(8,128)(2,1)} %copy-done.1, f32[4,128]{1,0:T(4,128)S(1)} %fusion.27, f32[4,128,2048]{2,1,0:T(8,128)} %copy-done.2), kind=kOutput, calls=%fused_computation.13 | convolution fusion | flops 1078200832 | bytes 13109248 | tf_op jit(solution)/shard_map/while/body/eval_jaxpr/rhk,rkl->rhl/dot_general | solution.py:70
  223.9 0.0 copy-start.3
  224.0 0.4 copy.54
  224.4 41.8 %all_to_all.53 = bf16[4,128,512]{2,0,1:T(4,128)(2,1)S(1)} all-to-all(bf16[4,128,512]{2,0,1:T(4,128)(2,1)S(1)} %copy.54), channel_id=1, replica_groups=mesh['grp'=16,'ctx'=32] {'ctx'}, dimensions={1} | all-to-all | bytes 1048576 | tf_op jit(solution)/shard_map/all_to_all | solution.py:78
  266.1 0.2 copy.63
  266.3 0.1 all_to_all.48
  266.4 0.0 copy-done.3
  266.5 0.3 fusion.10
  266.7 0.8 copy.56
  (14 shorter events, 0.2 us)
Async XLA Ops:
  0.0 13.3 %copy-start = (bf16[4,128,512]{2,1,0:T(8,128)(2,1)S(1)}, bf16[4,128,512]{2,1,0:T(8,128)(2,1)}, u32[]{:S(2)}) copy-start(bf16[4,128,512]{2,1,0:T(8,128)(2,1)} %param.6) | copy-start | bytes 1572868
  2.1 17.3 %all-to-all-start.1 = ((s32[32,1,4]{2,1,0:T(1,128)}), s32[32,1,4]{2,1,0:T(1,128)S(1)}, u32[]{:S(2)}, u32[]{:S(2)}) async-start(s32[32,1,4]{2,1,0:T(1,128)} %copy.46), calls=%async_computation.1 | async-start | bytes 32768 | tf_op jit(solution)/shard_map/all_to_all | solution.py:20
  19.5 23.7 %all-to-all-start = ((bf16[128,4,576]{2,1,0:T(4,128)(2,1)}), bf16[128,4,576]{2,1,0:T(4,128)(2,1)S(1)}, u32[]{:S(2)}, u32[]{:S(2)}) async-start(bf16[128,4,576]{2,1,0:T(4,128)(2,1)} %copy.42), calls=%async_computation | async-start | bytes 1310720 | tf_op jit(solution)/shard_map/all_to_all | solution.py:38
  43.2 7.8 %copy-start.4 = (s32[4,30]{1,0:T(4,128)S(1)}, s32[4,30]{1,0:T(4,128)}, u32[]{:S(2)}) copy-start(s32[4,30]{1,0:T(4,128)} %param.9) | copy-start | bytes 1444
  43.2 148.7 %all-to-all-start.2 = ((bf16[32,4,64,576]{3,2,1,0:T(8,128)(2,1)}), bf16[32,4,64,576]{3,2,1,0:T(8,128)(2,1)}, u32[]{:S(2)}, u32[]{:S(2)}) async-start(bf16[32,4,64,576]{3,2,1,0:T(8,128)(2,1)} %broadcast_select_fusion), calls=%async_computation.2 | async-start | bytes 20971520 | tf_op jit(solution)/shard_map/all_to_all | solution.py:22
  210.1 4.0 %copy-start.1 = (bf16[4,2048,576]{2,1,0:T(8,128)(2,1)}, bf16[4,2048,576]{2,1,0:T(8,128)(2,1)S(1)}, u32[]{:S(2)}) copy-start(bf16[4,2048,576]{2,1,0:T(8,128)(2,1)S(1)} %bitcast_select_fusion) | copy-start | bytes 28311556
  214.0 2.1 copy-start.2
  223.9 42.5 %copy-start.3 = (bf16[4,512,128]{2,1,0:T(8,128)(2,1)S(1)}, bf16[4,512,128]{2,1,0:T(8,128)(2,1)}, u32[]{:S(2)}) copy-start(bf16[4,512,128]{2,1,0:T(8,128)(2,1)} %param.7) | copy-start | bytes 1572868
where the time goes:
time: 268 us
  waiting for transfers between devices  142 us (53%)
  blocking collectives  41.8 us (16%)
  local copies, waits for them, and re-layouts  30 us (11%)
  starting transfers between devices  23.6 us (9%)
  other arithmetic  18.6 us (7%)
  matrix products  11.6 us (4%)
    all_to_all x1, waiting for transfers between devices, fetch_blocks(): lax.all_to_all(blocks, 'ctx', split_axis=0, concat_axis=0, tiled=True)  140 us
    all_to_all x1, blocking collectives, body(): lax.all_to_all(out_lat, 'ctx', split_axis=1, concat_axis=0, tiled=True)  41.8 us
    gather x1, local copies, waits for them, and re-layouts, attend_block(): jnp.take(fetched, pos_block, axis=0).reshape(q_block.shape[0], -1, width)  11.8 us
    all_to_all x1, starting transfers between devices, fetch_blocks(): lax.all_to_all(requests, 'ctx', split_axis=0, concat_axis=0, tiled=True)  10.4 us
    select_n x2, other arithmetic, fetch_blocks(): jnp.take(stored, lax.all_to_all(requests, 'ctx', split_axis=0, concat_axi...  10.1 us
    all_to_all x1, starting transfers between devices, fetch_blocks(): lax.all_to_all(blocks, 'ctx', split_axis=0, concat_axis=0, tiled=True)  7.57 us
    gather x1, local copies, waits for them, and re-layouts, fetch_blocks(): jnp.take(stored, lax.all_to_all(requests, 'ctx', split_axis=0, concat_axi...  7.4 us
    dot_general x1, matrix products, attend_block(): jnp.einsum('rhk,rkl->rhl', probs, keys[:, :, :DL], preferred_element_type...  6.52 us
  transfers between devices with their start and end apart: 3, of which 2 were waited for; matrix products, arithmetic and copies ran while one was open for 9% of the time, Pallas kernels for 0%

commit v1 on v0

v1 whole, which is shorter than its diff:
```python
import functools
import math

import jax
import jax.numpy as jnp
from jax import lax
from jax.experimental import pallas as pl
from jax.experimental.pallas import tpu as pltpu
from jax.sharding import PartitionSpec as P

MESH = pl.DeviceIdType.MESH
DL = 512
DN = 128
BLK = 64
ROWS = 144
N = 32
NEG = -1e30

RINGS = (
    ((2, 2),),
    ((2, 1), (2, 3), (1, 2), (3, 2)),
    ((2, 0), (0, 2)),
    ((1, 1), (3, 3), (1, 3), (3, 1)),
    ((1, 0), (3, 0), (0, 1), (0, 3)),
)
OFFSETS = [(0, 0, 0)]
for ring in RINGS:
    for core in (0, 1):
        OFFSETS += [(dx, dy, core) for dx, dy in ring]
OFFSETS.append((0, 0, 1))


def ahead(me, offset):
    dx, dy, dc = offset
    x, y, c = me // 8, (me // 2) % 4, me % 2
    return (((x + dx) % 4) * 4 + (y + dy) % 4) * 2 + (c + dc) % 2


def behind(me, offset):
    dx, dy, dc = offset
    return ahead(me, ((4 - dx) % 4, (4 - dy) % 4, dc))


def to(device):
    return dict(device_id={"ctx": device}, device_id_type=MESH)


def pack(cache, rope, id0, id1, put):
    put(pl.ds(0, BLK), pl.ds(0, DL), cache[id0, :, :DL])
    put(pl.ds(BLK, BLK), pl.ds(0, DL), cache[id1, :, :DL])
    lane = lax.broadcasted_iota(jnp.int32, (BLK, 128), 1)
    both = jnp.where(lane < 64, rope[id0], rope[id1])
    for k in range(4):
        put(pl.ds(2 * BLK, 16), pl.ds(128 * k, 128), both[16 * k : 16 * k + 16])


def kernel(
    query, absorb_k, absorb_v, cache, cold, out,
    rope, ids_out, ids_in, ids, bias, q_out, q_all, stage, keys, hot, extra,
    top, total, acc, lat_out, lat_in,
    ids_ss, ids_rs, q_ss, q_rs, k_ss, k_rs, o_ss, o_rs, hot_ss, hot_rs, id_sem,
):
    me = lax.axis_index("ctx")
    x, y, c = me // 8, (me // 2) % 4, me % 2
    barrier = pltpu.get_barrier_semaphore()
    for p in range(1, N):
        pl.semaphore_signal(barrier, inc=1, **to(ahead(me, OFFSETS[p])))

    base = lax.broadcasted_iota(jnp.int32, (N, 1), 0) * 16
    local = [cold[r : r + 1, :] - base for r in range(4)]
    low, high = None, None
    for r in range(4):
        inside = (local[r] >= 0) & (local[r] < 16)
        a = jnp.min(jnp.where(inside, local[r], 99), axis=1, keepdims=True)
        b = jnp.max(jnp.where(inside, local[r], -1), axis=1, keepdims=True)
        low = a if r == 0 else jnp.minimum(low, a)
        high = b if r == 0 else jnp.maximum(high, b)
    id0 = jnp.where(high < 0, 0, low)
    id1 = jnp.where(high < 0, 0, high)
    lane = lax.broadcasted_iota(jnp.int32, (N, 128), 1)
    ids_out[...] = jnp.where(lane == 0, id0, id1).reshape(N, 1, 128)
    for s, wanted in ((0, id0), (1, id1)):
        mark = jnp.zeros((N, 128), jnp.float32)
        for r in range(4):
            found = jnp.max(jnp.where(local[r] == wanted, 1, 0), axis=1, keepdims=True)
            if s == 1:
                found = jnp.where(id1 == id0, 0, found)
            mark = jnp.where((lane == r) & (found == 0), NEG, mark)
        bias[s] = mark

    pl.semaphore_wait(barrier, N - 1)
    id_copies = []
    for p in range(1, N):
        dst = ahead(me, OFFSETS[p])
        copy = pltpu.make_async_remote_copy(
            src_ref=ids_out.at[dst], dst_ref=ids_in.at[p], send_sem=ids_ss.at[p], recv_sem=ids_rs.at[p], **to(dst)
        )
        copy.start()
        id_copies.append(copy)

    doubled = jnp.concatenate([cache[:, :, DL:], cache[:, :, DL:]], axis=2)
    rope[...] = doubled

    def hot_copy(k, offset):
        return pltpu.make_async_remote_copy(
            src_ref=hot, dst_ref=hot, send_sem=hot_ss.at[k], recv_sem=hot_rs, **to(ahead(me, offset))
        )

    across = [hot_copy(d - 1, (d, 0, 0)) for d in (1, 2, 3)]
    down = [hot_copy(d + 2, (0, d, 0)) for d in (1, 2, 3)]
    over = hot_copy(6, (0, 0, 1))

    def put_hot(rows, columns, values):
        hot[rows, columns] = values

    @pl.when(me == N - 1)
    def _():
        pack(cache, rope, 14, 15, put_hot)
        for copy in across + down:
            copy.start()

    head = lax.broadcasted_iota(jnp.int32, (512, DN), 0) % 4
    plain = query[:, :DN]
    zero = jnp.zeros_like(plain)
    spread = jnp.concatenate([jnp.where(head == h, plain, zero) for h in range(4)], axis=1)
    q_out[:, :DL] = jnp.dot(spread, absorb_k[...], preferred_element_type=jnp.float32).astype(jnp.bfloat16)
    turn = query[:, DN:]
    q_out[:, DL:] = jnp.concatenate([turn, turn], axis=1)
    q_copies = []
    for p in range(1, N):
        dst = ahead(me, OFFSETS[p])
        copy = pltpu.make_async_remote_copy(
            src_ref=q_out.at[pl.ds(pl.multiple_of(dst * 16, 16), 16)],
            dst_ref=q_all.at[pl.ds(pl.multiple_of(me * 16, 16), 16), pl.ds(0, 640)],
            send_sem=q_ss.at[p], recv_sem=q_rs.at[p], **to(dst)
        )
        copy.start()
        q_copies.append(copy)

    @pl.when((y == 3) & (c == 1) & (x != 3))
    def _():
        across[0].wait_recv()
        for copy in down:
            copy.start()

    for p in range(1, N):
        id_copies[p - 1].wait_recv()
    fetch = pltpu.make_async_copy(ids_in, ids, id_sem)
    fetch.start()
    fetch.wait()
    k_copies = []
    for p in range(1, N):
        q = OFFSETS.index(((4 - OFFSETS[p][0]) % 4, (4 - OFFSETS[p][1]) % 4, OFFSETS[p][2]))
        dst = behind(me, OFFSETS[q])

        def put(rows, columns, values, p=p):
            stage[p, rows, columns] = values

        pack(cache, rope, ids[q, 0, 0], ids[q, 0, 1], put)
        copy = pltpu.make_async_remote_copy(
            src_ref=stage.at[p], dst_ref=keys.at[p], send_sem=k_ss.at[p], recv_sem=k_rs.at[p], **to(dst)
        )
        copy.start()
        k_copies.append(copy)

    @pl.when((c == 1) & (y != 3))
    def _():
        down[0].wait_recv()

    @pl.when(c == 1)
    def _():
        over.start()

    mine = pltpu.make_async_copy(ids_out.at[pl.ds(me, 1)], ids.at[pl.ds(0, 1)], id_sem)
    mine.start()
    mine.wait()

    def put_own(rows, columns, values):
        keys[0, rows, columns] = values

    pack(cache, rope, ids[0, 0, 0], ids[0, 0, 1], put_own)
    own = pl.ds(pl.multiple_of(me * 16, 16), 16)
    q_all[own, pl.ds(0, 640)] = q_out[own, :]
    marks = (lax.broadcasted_iota(jnp.int32, (512, 128), 0) // 4) % 4 == lax.broadcasted_iota(
        jnp.int32, (512, 128), 1
    )
    q_all[:, 640:] = jnp.where(marks, 1.0, 0.0).astype(jnp.bfloat16)
    for p in range(1, N):
        q_copies[p - 1].wait_recv()

    scale = math.log2(math.e) / math.sqrt(192)
    half = lax.broadcasted_iota(jnp.int32, (BLK, 128), 1) < 64
    none = jnp.zeros((BLK, 128), jnp.bfloat16)

    def unpack(tile, at, b0, b1):
        both = jnp.concatenate([tile[:, 128 * k : 128 * k + 128] for k in range(4)], axis=0)
        extra[pl.ds(at, BLK), pl.ds(0, 128)] = jnp.where(half, both, none)
        extra[pl.ds(at + BLK, BLK), pl.ds(0, 128)] = jnp.where(half, none, both)
        extra[pl.ds(at, BLK), pl.ds(128, 128)] = b0
        extra[pl.ds(at + BLK, BLK), pl.ds(128, 128)] = b1

    def scores(latent, tokens):
        dims = (((1,), (1,)), ((), ()))
        s = lax.dot_general(q_all[:, :DL], latent, dims, preferred_element_type=jnp.float32)
        s += lax.dot_general(q_all[:, DL:], extra[:tokens], dims, preferred_element_type=jnp.float32)
        return s * scale

    def add(latent, tokens):
        s = scores(latent, tokens)
        old = top[...]
        new = jnp.maximum(old, jnp.max(s, axis=1, keepdims=True))
        fade = jnp.exp2(old - new)
        w = jnp.exp2(s - new)
        total[...] = total[...] * fade + jnp.sum(w, axis=1, keepdims=True)
        top[...] = new
        acc[...] = acc[...] * fade + jnp.dot(
            w.astype(jnp.bfloat16), latent, preferred_element_type=jnp.float32
        )

    top[...] = jnp.full((512, 1), NEG, jnp.float32)
    total[...] = jnp.zeros((512, 1), jnp.float32)
    acc[...] = jnp.zeros((512, DL), jnp.float32)
    for chunk in range(8):
        for j in range(4):
            p = 4 * chunk + j
            if p:
                k_copies[p - 1].wait_recv()
            owner = behind(me, OFFSETS[p])
            b0 = jnp.broadcast_to(bias[0, pl.ds(owner, 1), :], (BLK, 128)).astype(jnp.bfloat16)
            b1 = jnp.broadcast_to(bias[1, pl.ds(owner, 1), :], (BLK, 128)).astype(jnp.bfloat16)
            unpack(keys[p, pl.ds(128, 16), :], 128 * j, b0, b1)
        add(keys[pl.ds(4 * chunk, 4), pl.ds(0, 128), :].reshape(512, DL), 512)
        if chunk == 0:
            @pl.when(c == 0)
            def _():
                over.wait_recv()

            unpack(hot[pl.ds(128, 16), :], 0, none, none)
            add(hot[pl.ds(0, 128), :], 128)

    lat_out[...] = (acc[...] / total[...]).astype(jnp.bfloat16)
    o_copies = []
    for p in range(1, N):
        dst = ahead(me, OFFSETS[p])
        copy = pltpu.make_async_remote_copy(
            src_ref=lat_out.at[pl.ds(pl.multiple_of(dst * 16, 16), 16)],
            dst_ref=lat_in.at[pl.ds(pl.multiple_of(me * 16, 16), 16)],
            send_sem=o_ss.at[p], recv_sem=o_rs.at[p], **to(dst)
        )
        copy.start()
        o_copies.append(copy)
    lat_in[own, :] = lat_out[own, :]
    for p in range(1, N):
        o_copies[p - 1].wait_recv()
    got = lat_in[...]
    result = jnp.zeros((512, 128), jnp.float32)
    for h in range(4):
        result = jnp.where(head == h, jnp.dot(got, absorb_v[h], preferred_element_type=jnp.float32), result)
    out[...] = result.astype(jnp.bfloat16)

    for copies in (id_copies, q_copies, k_copies, o_copies):
        for copy in copies:
            copy.wait_send()

    @pl.when(me == N - 1)
    def _():
        for copy in across:
            copy.wait_send()

    @pl.when((y == 3) & (c == 1))
    def _():
        for copy in down:
            copy.wait_send()

    @pl.when(c == 1)
    def _():
        over.wait_send()


def body(query, absorb_k, absorb_v, latent_cache, cold_blocks):
    vmem = pl.BlockSpec(memory_space=pltpu.VMEM)
    bf16, f32, i32 = jnp.bfloat16, jnp.float32, jnp.int32
    dma = pltpu.SemaphoreType.DMA
    out = pl.pallas_call(
        kernel,
        out_shape=jax.ShapeDtypeStruct((512, 128), bf16),
        in_specs=[vmem] * 5,
        out_specs=vmem,
        scratch_shapes=[
            pltpu.VMEM((16, BLK, 128), bf16),
            pltpu.VMEM((N, 1, 128), i32),
            pltpu.VMEM((N, 1, 128), i32),
            pltpu.SMEM((N, 1, 128), i32),
            pltpu.VMEM((2, N, 128), f32),
            pltpu.VMEM((512, 640), bf16),
            pltpu.VMEM((512, 768), bf16),
            pltpu.VMEM((N, ROWS, DL), bf16),
            pltpu.VMEM((N, ROWS, DL), bf16),
            pltpu.VMEM((ROWS, DL), bf16),
            pltpu.VMEM((512, 256), bf16),
            pltpu.VMEM((512, 1), f32),
            pltpu.VMEM((512, 1), f32),
            pltpu.VMEM((512, DL), f32),
            pltpu.VMEM((512, DL), bf16),
            pltpu.VMEM((512, DL), bf16),
        ]
        + [dma((N,))] * 8
        + [dma((7,)), dma, dma],
        compiler_params=pltpu.CompilerParams(collective_id=0, has_side_effects=True, vmem_limit_bytes=48 * 2**20),
    )(
        query.reshape(512, 192),
        absorb_k.reshape(512, DL),
        absorb_v,
        latent_cache.reshape(16, BLK, 576),
        cold_blocks,
    )
    return out.reshape(128, 4, 128)


def solution(mesh):
    placed = (
        P("grp", "ctx", None),
        P("ctx", None, None),
        P("ctx", None, None),
        P("ctx", None),
        P(("grp", "ctx"), None),
    )
    return jax.shard_map(
        body, mesh=mesh, in_specs=placed, out_specs=P("grp", "ctx", None), check_vma=False
    )
```

time: 268 us -> 96.6 us (0.36)
  waiting for transfers between devices: 142 us -> 0 us
  Pallas kernels: 0 us -> 92.7 us
  blocking collectives: 41.8 us -> 0 us
  local copies, waits for them, and re-layouts: 30 us -> 3.71 us
  starting transfers between devices: 23.6 us -> 0 us
  other arithmetic: 18.6 us -> 0 us
  matrix products: 11.6 us -> 0 us
    all_to_all x3 -> x0, waiting for transfers between devices: 142 us -> none  [the longest x1 140 us: fetch_blocks(): lax.all_to_all(blocks, 'ctx', split_axis=0, concat_axis=0, tiled=True)]
    pallas_call x0 -> x1, Pallas kernels: none -> 92.7 us  [body(): pl.pallas_call(kernel, out_shape=jax.ShapeDtypeStruct((512, 128), bf16),...]
    all_to_all x1 -> x0, blocking collectives: 41.8 us -> none  [body(): lax.all_to_all(out_lat, 'ctx', split_axis=1, concat_axis=0, tiled=True)]
    all_to_all x3 -> x0, starting transfers between devices: 23.6 us -> none  [the longest x1 10.4 us: fetch_blocks(): lax.all_to_all(requests, 'ctx', split_axis=0, concat_axis=0, tiled=True)]
    gather x2 -> x0, local copies, waits for them, and re-layouts: 19.2 us -> none  [the longest x1 11.8 us: attend_block(): jnp.take(fetched, pos_block, axis=0).reshape(q_block.shape[0], -1, width)]
    select_n x4 -> x0, other arithmetic: 16.6 us -> none  [the longest x2 10.1 us: fetch_blocks(): jnp.take(stored, lax.all_to_all(requests, 'ctx', split_axis=0, concat_axi...]
    dot_general x4 -> x0, matrix products: 11.6 us -> none  [the longest x1 6.52 us: attend_block(): jnp.einsum('rhk,rkl->rhl', probs, keys[:, :, :DL], preferred_element_type...]
  transfers between devices with their start and end apart: 3 -> 0, of which waited for: 2 -> 0; matrix products, arithmetic and copies ran while one was open for 9% -> 0% of each run, Pallas kernels for 0% -> 0%
where the time goes in v1:
time: 96.6 us; the launch traced here: 96.5 us
  Pallas kernels  92.7 us (96%)
  local copies, waits for them, and re-layouts  3.71 us (4%)
    pallas_call x1, Pallas kernels, body(): pl.pallas_call(kernel, out_shape=jax.ShapeDtypeStruct((512, 128), bf16),...  92.7 us
    unnamed x9, local copies, waits for them, and re-layouts  3.55 us

profile of v1, /device:TPU:1, one launch (start us, length us, event | category | flops | bytes accessed | tf_op | source)
XLA Modules:
  0.0 96.5 jit_solution(13147760935246518048)
XLA Ops:
  0.0 1.1 %copy.8 = bf16[128,4,192]{2,1,0:T(4,128)(2,1)S(1)} copy(bf16[128,4,192]{0,2,1:T(8,128)(2,1)} %param.5) | data formatting | bytes 393216 | tf_op args[0]
  1.1 0.2 reshape.12.query
  1.3 0.0 copy-start
  1.3 0.0 copy-start.1
  1.3 0.0 copy-start.2
  1.3 1.8 %copy.9 = bf16[1024,576]{1,0:T(8,128)(2,1)S(1)} copy(bf16[1024,576]{0,1:T(8,128)(2,1)} %param.8) | data formatting | bytes 2359296 | tf_op args[3]
  3.1 0.0 copy-done
  3.1 0.0 copy-done.1
  3.1 0.0 copy-done.2
  3.1 92.7 %shard_map.55 = bf16[512,128]{1,0:T(8,128)(2,1)S(1)} custom-call(bf16[512,192]{1,0:T(8,128)(2,1)S(1)} %reshape.12.query, bf16[512,512]{1,0:T(8,128)(2,1)S(1)} %bitcast.5, bf16[4,512,128]{2,1,0:T(8,128)(2,1)S(1)} %copy-done.1, bf16[16,64,576]{2,1,0:T(8,128)(2,1)S(1)} %bitcast.3, s32[4,30]{1,0:T(4,128)S(1)} %copy-done.2), custom_call_target="tpu_custom_call" | custom-call | tf_op jit(solution)/shard_map/pallas_call | solution.py:284
  95.8 0.7 copy.11
Async XLA Ops:
  1.3 1.8 %copy-start = (bf16[4,128,512]{2,1,0:T(8,128)(2,1)S(1)}, bf16[4,128,512]{2,1,0:T(8,128)(2,1)}, u32[]{:S(2)}) copy-start(bf16[4,128,512]{2,1,0:T(8,128)(2,1)} %param.6) | copy-start | bytes 1572868
  1.3 1.8 %copy-start.1 = (bf16[4,512,128]{2,1,0:T(8,128)(2,1)S(1)}, bf16[4,512,128]{2,1,0:T(8,128)(2,1)}, u32[]{:S(2)}) copy-start(bf16[4,512,128]{2,1,0:T(8,128)(2,1)} %absorb_v.1) | copy-start | bytes 1572868
  1.3 1.8 %copy-start.2 = (s32[4,30]{1,0:T(4,128)S(1)}, s32[4,30]{1,0:T(4,128)}, u32[]{:S(2)}) copy-start(s32[4,30]{1,0:T(4,128)} %cold.1) | copy-start | bytes 1444

commit v2 on v1

v2 whole, which is shorter than its diff:
```python
import functools
import math

import jax
import jax.numpy as jnp
from jax import lax
from jax.experimental import pallas as pl
from jax.experimental.pallas import tpu as pltpu
from jax.sharding import PartitionSpec as P

MESH = pl.DeviceIdType.MESH
DL = 512
DN = 128
BLK = 64
QUARTER = 32
PARTS = 4
N = 32
NEG = -1e30

RINGS = (
    ((1, 1), (3, 3), (1, 3), (3, 1)),
    ((2, 1), (0, 1), (2, 3), (0, 3)),
    ((2, 2),),
    ((1, 2), (1, 0), (3, 2), (3, 0)),
    ((2, 0), (0, 2)),
)
OFFSETS = [(0, 0, 0)]
for ring in RINGS:
    for core in (0, 1):
        OFFSETS += [(dx, dy, core) for dx, dy in ring]
OFFSETS.append((0, 0, 1))


def ahead(me, offset):
    dx, dy, dc = offset
    x, y, c = me // 8, (me // 2) % 4, me % 2
    return (((x + dx) % 4) * 4 + (y + dy) % 4) * 2 + (c + dc) % 2


def behind(me, offset):
    dx, dy, dc = offset
    return ahead(me, ((4 - dx) % 4, (4 - dy) % 4, dc))


def to(device):
    return dict(device_id={"ctx": device}, device_id_type=MESH)


def pack(cache, rope, id0, id1, latents, turns):
    for k in range(PARTS):
        latents[k][...] = cache[id0 if k < 2 else id1, pl.ds(QUARTER * (k % 2), QUARTER), :]
    lane = lax.broadcasted_iota(jnp.int32, (BLK, 128), 1)
    both = jnp.where(lane < 64, rope[id0], rope[id1])
    for b in range(4):
        turns[:, pl.ds(128 * b, 128)] = both[16 * b : 16 * b + 16]


def kernel(
    query_at, absorb_k_at, absorb_v_at, stored_at, cold, out,
    query, absorb_k, absorb_v, stored,
    cache, rope, ids_out, ids_in, ids, bias, q_out, q_all, stage, stage_turn, keys, keys_turn, hot, hot_turn, extra,
    top, total, acc, lat_out, lat_in,
    ids_ss, ids_rs, q_ss, q_rs, k_ss, k_rs, t_ss, t_rs, o_ss, o_rs, hot_ss, hot_rs, id_sem, in_sem,
):
    me = lax.axis_index("ctx")
    x, y, c = me // 8, (me // 2) % 4, me % 2
    barrier = pltpu.get_barrier_semaphore()
    for p in range(1, N):
        pl.semaphore_signal(barrier, inc=1, **to(ahead(me, OFFSETS[p])))

    loads = [
        pltpu.make_async_copy(src, dst, in_sem.at[k])
        for k, (src, dst) in enumerate(
            ((stored_at, stored), (query_at, query), (absorb_k_at, absorb_k), (absorb_v_at, absorb_v))
        )
    ]
    for load in loads:
        load.start()

    base = lax.broadcasted_iota(jnp.int32, (N, 1), 0) * 16
    local = [cold[r : r + 1, :] - base for r in range(4)]
    low, high = None, None
    for r in range(4):
        inside = (local[r] >= 0) & (local[r] < 16)
        a = jnp.min(jnp.where(inside, local[r], 99), axis=1, keepdims=True)
        b = jnp.max(jnp.where(inside, local[r], -1), axis=1, keepdims=True)
        low = a if r == 0 else jnp.minimum(low, a)
        high = b if r == 0 else jnp.maximum(high, b)
    id0 = jnp.where(high < 0, 0, low)
    id1 = jnp.where(high < 0, 0, high)
    lane = lax.broadcasted_iota(jnp.int32, (N, 128), 1)
    ids_out[...] = jnp.where(lane == 0, id0, id1).reshape(N, 1, 128)
    for s, wanted in ((0, id0), (1, id1)):
        mark = jnp.zeros((N, 128), jnp.float32)
        for r in range(4):
            found = jnp.max(jnp.where(local[r] == wanted, 1, 0), axis=1, keepdims=True)
            if s == 1:
                found = jnp.where(id1 == id0, 0, found)
            mark = jnp.where((lane == r) & (found == 0), NEG, mark)
        bias[s] = mark

    pl.semaphore_wait(barrier, N - 1)
    for p in range(1, N):
        dst = ahead(me, OFFSETS[p])
        pltpu.make_async_remote_copy(
            src_ref=ids_out.at[dst], dst_ref=ids_in.at[p], send_sem=ids_ss, recv_sem=ids_rs, **to(dst)
        ).start()

    def settled(ref, sends, lands):
        return pltpu.make_async_remote_copy(src_ref=ref, dst_ref=ref, send_sem=sends, recv_sem=lands, **to(ahead(me, OFFSETS[1])))

    lanes = (((1,), (1,)), ((), ()))
    unit = jnp.where(
        lax.broadcasted_iota(jnp.int32, (256, 256), 0) == lax.broadcasted_iota(jnp.int32, (256, 256), 1), 1.0, 0.0
    ).astype(jnp.bfloat16)
    loads[0].wait()
    for k in range(4):
        part = pl.ds(256 * k, 256)
        turned = lax.dot_general(unit, stored[:DL, part], lanes, preferred_element_type=jnp.float32)
        cache[pl.ds(4 * k, 4)] = turned.astype(jnp.bfloat16).reshape(4, BLK, DL)
        tail = stored[DL:, part]
        turned = lax.dot_general(
            unit, jnp.concatenate([tail, tail], axis=0), lanes, preferred_element_type=jnp.float32
        )
        rope[pl.ds(4 * k, 4)] = turned.astype(jnp.bfloat16).reshape(4, BLK, 128)

    def hot_copies(k, offset):
        device = to(ahead(me, offset))
        return [
            pltpu.make_async_remote_copy(
                src_ref=ref, dst_ref=ref, send_sem=hot_ss.at[i, k], recv_sem=hot_rs.at[i], **device
            )
            for i, ref in enumerate((hot, hot_turn))
        ]

    across = hot_copies(0, (1, 0, 0)) + hot_copies(1, (2, 0, 0)) + hot_copies(2, (3, 0, 0))
    down = hot_copies(3, (0, 1, 0)) + hot_copies(4, (0, 2, 0)) + hot_copies(5, (0, 3, 0))
    over = hot_copies(6, (0, 0, 1))

    @pl.when(me == N - 1)
    def _():
        pack(cache, rope, 14, 15, [hot.at[k] for k in range(PARTS)], hot_turn)
        for copy in across + down:
            copy.start()

    row = lax.broadcasted_iota(jnp.int32, (512, 128), 0)
    column = lax.broadcasted_iota(jnp.int32, (512, 128), 1)
    plain, turn = [], None
    loads[1].wait()
    loads[2].wait()
    for h in range(4):
        pick = jnp.where(row == 4 * column + h, 1.0, 0.0).astype(jnp.bfloat16)
        spread = lax.dot_general(pick, query[h], lanes, preferred_element_type=jnp.float32)
        plain.append(spread[:, :DN].astype(jnp.bfloat16))
        turn = spread[:, DN:] if h == 0 else turn + spread[:, DN:]
    q_out[:, :DL] = jnp.dot(
        jnp.concatenate(plain, axis=1), absorb_k[...], preferred_element_type=jnp.float32
    ).astype(jnp.bfloat16)
    turn = turn.astype(jnp.bfloat16)
    q_out[:, DL:] = jnp.concatenate([turn, turn], axis=1)
    for p in range(1, N):
        dst = ahead(me, OFFSETS[p])
        pltpu.make_async_remote_copy(
            src_ref=q_out.at[pl.ds(pl.multiple_of(dst * 16, 16), 16)],
            dst_ref=q_all.at[pl.ds(16 * p, 16), pl.ds(0, 640)],
            send_sem=q_ss, recv_sem=q_rs, **to(dst)
        ).start()

    settled(ids_in.at[pl.ds(1, N - 1)], ids_ss, ids_rs).wait_recv()
    fetch = pltpu.make_async_copy(ids_in, ids, id_sem)
    fetch.start()
    fetch.wait()

    def send_part(k, p):
        pltpu.make_async_remote_copy(
            src_ref=stage.at[k, p], dst_ref=keys.at[k, p], send_sem=k_ss.at[k], recv_sem=k_rs.at[k, p // 16],
            **to(ahead(me, OFFSETS[p]))
        ).start()

    for p in range(1, N):
        q = OFFSETS.index(((4 - OFFSETS[p][0]) % 4, (4 - OFFSETS[p][1]) % 4, OFFSETS[p][2]))
        pack(
            cache, rope, ids[q, 0, 0], ids[q, 0, 1], [stage.at[k, p] for k in range(PARTS)], stage_turn.at[p]
        )
        pltpu.make_async_remote_copy(
            src_ref=stage_turn.at[p], dst_ref=keys_turn.at[p], send_sem=t_ss, recv_sem=t_rs,
            **to(ahead(me, OFFSETS[p]))
        ).start()
        send_part(0, p)

    @pl.when((y == 3) & (c == 1) & (x != 3))
    def _():
        for copy in across[:2]:
            copy.wait_recv()
        for copy in down:
            copy.start()

    for p in range(1, N):
        send_part(1, p)

    @pl.when((c == 1) & (y != 3))
    def _():
        for copy in down[:2]:
            copy.wait_recv()

    @pl.when(c == 1)
    def _():
        for copy in over:
            copy.start()

    for k in (2, 3):
        for p in range(1, N):
            send_part(k, p)

    mine = pltpu.make_async_copy(ids_out.at[pl.ds(me, 1)], ids.at[pl.ds(0, 1)], id_sem)
    mine.start()
    mine.wait()

    pack(cache, rope, ids[0, 0, 0], ids[0, 0, 1], [keys.at[k, 0] for k in range(PARTS)], keys_turn.at[0])
    own = pl.ds(pl.multiple_of(me * 16, 16), 16)
    q_all[pl.ds(0, 16), pl.ds(0, 640)] = q_out[own, :]
    marks = (lax.broadcasted_iota(jnp.int32, (512, 128), 0) // 4) % 4 == lax.broadcasted_iota(
        jnp.int32, (512, 128), 1
    )
    q_all[:, 640:] = jnp.where(marks, 1.0, 0.0).astype(jnp.bfloat16)
    for p in range(N):
        owner = behind(me, OFFSETS[p])
        for s in range(2):
            wide = jnp.broadcast_to(bias[s, pl.ds(owner, 1), :], (QUARTER, 128)).astype(jnp.bfloat16)
            for k in (2 * s, 2 * s + 1):
                extra[k, p, :, pl.ds(128, 128)] = wide
    settled(q_all.at[pl.ds(16, 496), pl.ds(0, 640)], q_ss, q_rs).wait_recv()

    scale = math.log2(math.e) / math.sqrt(192)
    first = lax.broadcasted_iota(jnp.int32, (QUARTER, 128), 1) < 64
    none = jnp.zeros((QUARTER, 128), jnp.bfloat16)

    def unpack(turns, put):
        for b in range(2):
            both = jnp.concatenate([turns[:, 256 * b + 128 * i : 256 * b + 128 * i + 128] for i in range(2)], axis=0)
            put(b, jnp.where(first, both, none))
            put(2 + b, jnp.where(first, none, both))

    def scores(latent, more):
        s = lax.dot_general(q_all[:, :DL], latent, lanes, preferred_element_type=jnp.float32)
        s += lax.dot_general(q_all[:, DL:], more, lanes, preferred_element_type=jnp.float32)
        return s * scale

    def add(latent, more):
        s = scores(latent, more)
        old = top[...]
        new = jnp.maximum(old, jnp.max(s, axis=1, keepdims=True))
        fade = jnp.exp2(old - new)
        w = jnp.exp2(s - new)
        total[...] = total[...] * fade + jnp.sum(w, axis=1, keepdims=True)
        top[...] = new
        acc[...] = acc[...] * fade + jnp.dot(
            w.astype(jnp.bfloat16), latent, preferred_element_type=jnp.float32
        )

    top[...] = jnp.full((512, 1), NEG, jnp.float32)
    total[...] = jnp.zeros((512, 1), jnp.float32)
    acc[...] = jnp.zeros((512, DL), jnp.float32)

    @pl.when(c == 0)
    def _():
        for copy in over:
            copy.wait_recv()

    hot_more = []
    unpack(hot_turn[...], lambda k, values: hot_more.append((k, values)))
    hot_more = jnp.concatenate([values for _, values in sorted(hot_more, key=lambda item: item[0])], axis=0)
    add(hot[...].reshape(128, DL), jnp.concatenate([hot_more, jnp.zeros_like(hot_more)], axis=1))

    settled(keys_turn.at[pl.ds(1, N - 1)], t_ss, t_rs).wait_recv()
    for p in range(N):

        def put(k, values, p=p):
            extra[k, p, :, pl.ds(0, 128)] = values

        unpack(keys_turn[p], put)
    for k in range(PARTS):
        for j in range(2):
            settled(keys.at[k, pl.ds(1, 15) if j == 0 else pl.ds(16, 16)], k_ss.at[k], k_rs.at[k, j]).wait_recv()
            run = pl.ds(16 * j, 16)
            add(keys[k, run].reshape(512, DL), extra[k, run].reshape(512, 256))

    lat_out[...] = (acc[...] / total[...]).astype(jnp.bfloat16)
    for p in range(1, N):
        dst = behind(me, OFFSETS[p])
        pltpu.make_async_remote_copy(
            src_ref=lat_out.at[pl.ds(16 * p, 16)],
            dst_ref=lat_in.at[pl.ds(pl.multiple_of(me * 16, 16), 16)],
            send_sem=o_ss, recv_sem=o_rs, **to(dst)
        ).start()
    lat_in[own, :] = lat_out[pl.ds(0, 16), :]
    settled(lat_in.at[pl.ds(0, 496)], o_ss, o_rs).wait_recv()
    loads[3].wait()
    got = lat_in[...]
    result = jnp.zeros((512, 128), jnp.float32)
    for h in range(4):
        result = jnp.where(row % 4 == h, jnp.dot(got, absorb_v[h], preferred_element_type=jnp.float32), result)
    out[...] = result.astype(jnp.bfloat16)

    settled(ids_in.at[pl.ds(1, N - 1)], ids_ss, ids_rs).wait_send()
    settled(q_out.at[pl.ds(0, 496)], q_ss, q_rs).wait_send()
    settled(stage_turn.at[pl.ds(1, N - 1)], t_ss, t_rs).wait_send()
    for k in range(PARTS):
        settled(stage.at[k, pl.ds(1, N - 1)], k_ss.at[k], k_rs.at[k, 0]).wait_send()
    settled(lat_out.at[pl.ds(0, 496)], o_ss, o_rs).wait_send()

    @pl.when(me == N - 1)
    def _():
        for copy in across:
            copy.wait_send()

    @pl.when((y == 3) & (c == 1))
    def _():
        for copy in down:
            copy.wait_send()

    @pl.when(c == 1)
    def _():
        for copy in over:
            copy.wait_send()


def body(query, absorb_k, absorb_v, latent_cache, cold_blocks):
    vmem = pl.BlockSpec(memory_space=pltpu.VMEM)
    bf16, f32, i32 = jnp.bfloat16, jnp.float32, jnp.int32
    dma = pltpu.SemaphoreType.DMA
    out = pl.pallas_call(
        kernel,
        out_shape=jax.ShapeDtypeStruct((512, 128), bf16),
        in_specs=[pl.BlockSpec(memory_space=pl.ANY)] * 4 + [vmem],
        out_specs=vmem,
        scratch_shapes=[
            pltpu.VMEM((4, 192, 128), bf16),
            pltpu.VMEM((512, DL), bf16),
            pltpu.VMEM((4, DL, 128), bf16),
            pltpu.VMEM((576, 1024), bf16),
            pltpu.VMEM((16, BLK, DL), bf16),
            pltpu.VMEM((16, BLK, 128), bf16),
            pltpu.VMEM((N, 1, 128), i32),
            pltpu.VMEM((N, 1, 128), i32),
            pltpu.SMEM((N, 1, 128), i32),
            pltpu.VMEM((2, N, 128), f32),
            pltpu.VMEM((512, 640), bf16),
            pltpu.VMEM((512, 768), bf16),
            pltpu.VMEM((PARTS, N, QUARTER, DL), bf16),
            pltpu.VMEM((N, 16, DL), bf16),
            pltpu.VMEM((PARTS, N, QUARTER, DL), bf16),
            pltpu.VMEM((N, 16, DL), bf16),
            pltpu.VMEM((PARTS, QUARTER, DL), bf16),
            pltpu.VMEM((16, DL), bf16),
            pltpu.VMEM((PARTS, N, QUARTER, 256), bf16),
            pltpu.VMEM((512, 1), f32),
            pltpu.VMEM((512, 1), f32),
            pltpu.VMEM((512, DL), f32),
            pltpu.VMEM((512, DL), bf16),
            pltpu.VMEM((512, DL), bf16),
        ]
        + [dma, dma, dma, dma, dma((PARTS,)), dma((PARTS, 2)), dma, dma, dma, dma]
        + [dma((2, 7)), dma((2,)), dma, dma((4,))],
        compiler_params=pltpu.CompilerParams(collective_id=0, has_side_effects=True, vmem_limit_bytes=64 * 2**20 - 160 * 2**10),
    )(
        query.transpose(1, 2, 0),
        absorb_k.reshape(512, DL),
        absorb_v,
        latent_cache.T,
        cold_blocks,
    )
    return out.reshape(128, 4, 128)


def solution(mesh):
    placed = (
        P("grp", "ctx", None),
        P("ctx", None, None),
        P("ctx", None, None),
        P("ctx", None),
        P(("grp", "ctx"), None),
    )
    return jax.shard_map(
        body, mesh=mesh, in_specs=placed, out_specs=P("grp", "ctx", None), check_vma=False
    )
```

time: 96.6 us -> 93.5 us (0.968)
  local copies, waits for them, and re-layouts: 3.71 us -> 1.61 us
  Pallas kernels: 92.7 us -> 91.7 us
    unnamed x9 -> x1, local copies, waits for them, and re-layouts: 3.55 us -> 1.61 us
    pallas_call x1, Pallas kernels: 92.7 us -> 91.7 us  [body(): pl.pallas_call(kernel, out_shape=jax.ShapeDtypeStruct((512, 128), bf16),...]
where the time goes in v2:
time: 93.5 us; the launch traced here: 93.3 us
  Pallas kernels  91.7 us (98%)
  local copies, waits for them, and re-layouts  1.61 us (2%)
    pallas_call x1, Pallas kernels, body(): pl.pallas_call(kernel, out_shape=jax.ShapeDtypeStruct((512, 128), bf16),...  91.7 us

profile of v2, /device:TPU:1, one launch (start us, length us, event | category | flops | bytes accessed | tf_op | source)
XLA Modules:
  0.0 93.3 jit_solution(15163090728595713665)
XLA Ops:
  0.0 91.7 %shard_map.55 = bf16[512,128]{1,0:T(8,128)(2,1)} custom-call(bf16[4,192,128]{2,1,0:T(8,128)(2,1)} %bitcast.7, bf16[512,512]{1,0:T(8,128)(2,1)} %bitcast.6, bf16[4,512,128]{2,1,0:T(8,128)(2,1)} %absorb_v_at.1, bf16[576,1024]{1,0:T(8,128)(2,1)} %bitcast.4, s32[4,30]{1,0:T(4,128)} %cold.1), custom_call_target="tpu_custom_call" | custom-call | tf_op jit(solution)/shard_map/pallas_call | solution.py:332
  91.7 1.6 %copy.7 = bf16[128,4,128]{2,1,0:T(4,128)(2,1)} copy(bf16[128,4,128]{2,1,0:T(4,128)(2,1)} %bitcast.5) | data formatting | bytes 262144

commit v3 on v2

--- a/solution.py
+++ b/solution.py
@@ -12,10 +12,11 @@
 DL = 512
 DN = 128
 BLK = 64
-QUARTER = 32
-PARTS = 4
 N = 32
 NEG = -1e30
+
+AXIS = (0, 3, 1, 2)
+SERVED = ((0, 1), (0, 3), (0, 2), (1, 1), (1, 3), (1, 2), (1, 0))
 
 RINGS = (
     ((1, 1), (3, 3), (1, 3), (3, 1)),
@@ -46,9 +47,9 @@
     return dict(device_id={"ctx": device}, device_id_type=MESH)
 
 
-def pack(cache, rope, id0, id1, latents, turns):
-    for k in range(PARTS):
-        latents[k][...] = cache[id0 if k < 2 else id1, pl.ds(QUARTER * (k % 2), QUARTER), :]
+def pack(rows, rope, id0, id1, first, second, turns):
+    first[...] = rows[id0]
+    second[...] = rows[id1]
     lane = lax.broadcasted_iota(jnp.int32, (BLK, 128), 1)
     both = jnp.where(lane < 64, rope[id0], rope[id1])
     for b in range(4):
@@ -58,12 +59,31 @@
 def kernel(
     query_at, absorb_k_at, absorb_v_at, stored_at, cold, out,
     query, absorb_k, absorb_v, stored,
-    cache, rope, ids_out, ids_in, ids, bias, q_out, q_all, stage, stage_turn, keys, keys_turn, hot, hot_turn, extra,
+    rows0, rows1, rows2, rows3, rope, pairs, ids_out, ids_in, ids, bias, q_out, q_all, stage, stage_turn, keys, keys_turn, hot, hot_turn, extra,
     top, total, acc, lat_out, lat_in,
-    ids_ss, ids_rs, q_ss, q_rs, k_ss, k_rs, t_ss, t_rs, o_ss, o_rs, hot_ss, hot_rs, id_sem, in_sem,
+    ids_ss, ids_rs, own_ss, own_rs, fwd_ss, fwd_rs, q_ss, q_rs, k_ss, k_rs, t_ss, t_rs, o_ss, o_rs, hot_ss, hot_rs, id_sem, in_sem,
 ):
     me = lax.axis_index("ctx")
     x, y, c = me // 8, (me // 2) % 4, me % 2
+
+    def place(core):
+        return jnp.where(core == 0, y, x), jnp.where(core == 0, x, y)
+
+    def device(core, u, v):
+        return (jnp.where(core == 0, v, u) * 4 + jnp.where(core == 0, u, v)) * 2 + core
+
+    u, v = place(c)
+    rows = (rows0, rows1, rows2, rows3)
+    plus, minus = device(c, u, (v + 1) % 4), device(c, u, (v + 3) % 4)
+
+    def served(flip, e):
+        return device(c, (u + e) % 4, v) - c + (c + flip) % 2
+
+    def server(flip, e):
+        core = (c + flip) % 2
+        cu, cv = place(core)
+        return device(core, (cu + 4 - e) % 4, cv), core * 16 + (cu + 4 - e) % 4 * 4, cv
+
     barrier = pltpu.get_barrier_semaphore()
     for p in range(1, N):
         pl.semaphore_signal(barrier, inc=1, **to(ahead(me, OFFSETS[p])))
@@ -77,7 +97,9 @@
     for load in loads:
         load.start()
 
-    base = lax.broadcasted_iota(jnp.int32, (N, 1), 0) * 16
+    line = lax.broadcasted_iota(jnp.int32, (N, 1), 0)
+    core, cu, cv = line // 16, (line // 4) % 4, line % 4
+    base = jnp.where(core == 0, cv * 8 + cu * 2, cu * 8 + cv * 2 + 1) * 16
     local = [cold[r : r + 1, :] - base for r in range(4)]
     low, high = None, None
     for r in range(4):
@@ -99,16 +121,6 @@
             mark = jnp.where((lane == r) & (found == 0), NEG, mark)
         bias[s] = mark
 
-    pl.semaphore_wait(barrier, N - 1)
-    for p in range(1, N):
-        dst = ahead(me, OFFSETS[p])
-        pltpu.make_async_remote_copy(
-            src_ref=ids_out.at[dst], dst_ref=ids_in.at[p], send_sem=ids_ss, recv_sem=ids_rs, **to(dst)
-        ).start()
-
-    def settled(ref, sends, lands):
-        return pltpu.make_async_remote_copy(src_ref=ref, dst_ref=ref, send_sem=sends, recv_sem=lands, **to(ahead(me, OFFSETS[1])))
-
     lanes = (((1,), (1,)), ((), ()))
     unit = jnp.where(
         lax.broadcasted_iota(jnp.int32, (256, 256), 0) == lax.broadcasted_iota(jnp.int32, (256, 256), 1), 1.0, 0.0
@@ -117,12 +129,26 @@
     for k in range(4):
         part = pl.ds(256 * k, 256)
         turned = lax.dot_general(unit, stored[:DL, part], lanes, preferred_element_type=jnp.float32)
-        cache[pl.ds(4 * k, 4)] = turned.astype(jnp.bfloat16).reshape(4, BLK, DL)
+        rows[0][pl.ds(4 * k, 4)] = turned.astype(jnp.bfloat16).reshape(4, BLK, DL)
         tail = stored[DL:, part]
         turned = lax.dot_general(
             unit, jnp.concatenate([tail, tail], axis=0), lanes, preferred_element_type=jnp.float32
         )
-        rope[pl.ds(4 * k, 4)] = turned.astype(jnp.bfloat16).reshape(4, BLK, 128)
+        rope[0, pl.ds(4 * k, 4)] = turned.astype(jnp.bfloat16).reshape(4, BLK, 128)
+    low_lanes = lax.broadcasted_iota(jnp.int32, (8, BLK, 128), 2) < 64
+    pairs[0] = jnp.where(low_lanes, rope[0, pl.ds(0, 8)], rope[0, pl.ds(8, 8)])
+
+    pl.semaphore_wait(barrier, N - 1)
+    for flip, e in SERVED:
+        there, first_row, _ = server(flip, e)
+        pltpu.make_async_remote_copy(
+            src_ref=ids_out.at[pl.ds(first_row, 4)], dst_ref=ids_in.at[4 * flip + e],
+            send_sem=ids_ss, recv_sem=ids_rs, **to(there)
+        ).start()
+    ids_in[0] = ids_out[pl.ds(c * 16 + u * 4, 4)]
+
+    def settled(ref, sends, lands):
+        return pltpu.make_async_remote_copy(src_ref=ref, dst_ref=ref, send_sem=sends, recv_sem=lands, **to(ahead(me, OFFSETS[1])))
 
     def hot_copies(k, offset):
         device = to(ahead(me, offset))
@@ -139,9 +165,37 @@
 
     @pl.when(me == N - 1)
     def _():
-        pack(cache, rope, 14, 15, [hot.at[k] for k in range(PARTS)], hot_turn)
+        pack(rows[0], rope.at[0], 14, 15, hot.at[0], hot.at[1], hot_turn)
         for copy in across + down:
             copy.start()
+
+    def hop(src, dst, half, there, sends, lands):
+        span, turns = pl.ds(8 * half, 8), pl.ds(4 * half, 4)
+        return [
+            pltpu.make_async_remote_copy(
+                src_ref=a, dst_ref=b, send_sem=sends.at[i], recv_sem=lands.at[i], **to(there)
+            )
+            for i, (a, b) in enumerate(
+                ((rows[src].at[span], rows[dst].at[span]), (pairs.at[src, turns], pairs.at[dst, turns]))
+            )
+        ]
+
+    own_up = [hop(0, 1, h, plus, own_ss.at[0, h], own_rs.at[0, h]) for h in (0, 1)]
+    own_down = [hop(0, 2, h, minus, own_ss.at[1, h], own_rs.at[1, h]) for h in (0, 1)]
+    on_up = hop(1, 3, 0, plus, fwd_ss.at[0], fwd_rs.at[0])
+    on_down = hop(2, 3, 1, minus, fwd_ss.at[1], fwd_rs.at[1])
+
+    def start(*groups):
+        for copies in groups:
+            for copy in copies:
+                copy.start()
+
+    def arrive(*groups):
+        for copies in groups:
+            for copy in copies:
+                copy.wait_recv()
+
+    start(own_up[0], own_down[1])
 
     row = lax.broadcasted_iota(jnp.int32, (512, 128), 0)
     column = lax.broadcasted_iota(jnp.int32, (512, 128), 1)
@@ -166,80 +220,95 @@
             send_sem=q_ss, recv_sem=q_rs, **to(dst)
         ).start()
 
-    settled(ids_in.at[pl.ds(1, N - 1)], ids_ss, ids_rs).wait_recv()
+    @pl.when((y == 3) & (c == 1) & (x != 3))
+    def _():
+        arrive(across[:2])
+        start(down)
+
+    start(own_up[1], own_down[0])
+
+    settled(ids_in.at[pl.ds(1, 7)], ids_ss, ids_rs).wait_recv()
     fetch = pltpu.make_async_copy(ids_in, ids, id_sem)
     fetch.start()
     fetch.wait()
 
-    def send_part(k, p):
-        pltpu.make_async_remote_copy(
-            src_ref=stage.at[k, p], dst_ref=keys.at[k, p], send_sem=k_ss.at[k], recv_sem=k_rs.at[k, p // 16],
-            **to(ahead(me, OFFSETS[p]))
-        ).start()
-
-    for p in range(1, N):
-        q = OFFSETS.index(((4 - OFFSETS[p][0]) % 4, (4 - OFFSETS[p][1]) % 4, OFFSETS[p][2]))
+    def serve(w):
+        at = (v + AXIS[w]) % 4
+        for flip, e in SERVED:
+            j = 4 * flip + e
+            pack(
+                rows[w], rope.at[w], ids[j, at, 0, 0], ids[j, at, 0, 1],
+                stage.at[w, 0, j], stage.at[w, 1, j], stage_turn.at[w, j]
+            )
+            there = to(served(flip, e))
+            pltpu.make_async_remote_copy(
+                src_ref=stage_turn.at[w, j], dst_ref=keys_turn.at[w, j],
+                send_sem=t_ss.at[w], recv_sem=t_rs.at[w], **there
+            ).start()
+            pltpu.make_async_remote_copy(
+                src_ref=stage.at[w, 0, j], dst_ref=keys.at[w, 0, j],
+                send_sem=k_ss.at[w, 0], recv_sem=k_rs.at[w, 0], **there
+            ).start()
+        for flip, e in SERVED:
+            j = 4 * flip + e
+            pltpu.make_async_remote_copy(
+                src_ref=stage.at[w, 1, j], dst_ref=keys.at[w, 1, j],
+                send_sem=k_ss.at[w, 1], recv_sem=k_rs.at[w, 1], **to(served(flip, e))
+            ).start()
         pack(
-            cache, rope, ids[q, 0, 0], ids[q, 0, 1], [stage.at[k, p] for k in range(PARTS)], stage_turn.at[p]
+            rows[w], rope.at[w], ids[0, at, 0, 0], ids[0, at, 0, 1],
+            keys.at[w, 0, 0], keys.at[w, 1, 0], keys_turn.at[w, 0]
         )
-        pltpu.make_async_remote_copy(
-            src_ref=stage_turn.at[p], dst_ref=keys_turn.at[p], send_sem=t_ss, recv_sem=t_rs,
-            **to(ahead(me, OFFSETS[p]))
-        ).start()
-        send_part(0, p)
-
-    @pl.when((y == 3) & (c == 1) & (x != 3))
-    def _():
-        for copy in across[:2]:
-            copy.wait_recv()
-        for copy in down:
-            copy.start()
-
-    for p in range(1, N):
-        send_part(1, p)
-
-    @pl.when((c == 1) & (y != 3))
-    def _():
-        for copy in down[:2]:
-            copy.wait_recv()
-
-    @pl.when(c == 1)
-    def _():
-        for copy in over:
-            copy.start()
-
-    for k in (2, 3):
-        for p in range(1, N):
-            send_part(k, p)
-
-    mine = pltpu.make_async_copy(ids_out.at[pl.ds(me, 1)], ids.at[pl.ds(0, 1)], id_sem)
-    mine.start()
-    mine.wait()
-
-    pack(cache, rope, ids[0, 0, 0], ids[0, 0, 1], [keys.at[k, 0] for k in range(PARTS)], keys_turn.at[0])
+
+    def widen(w):
+        both = pairs[w]
+        for half in (0, 1):
+            one = both[:, :, 64 * half : 64 * half + 64]
+            rope[w, pl.ds(8 * half, 8)] = jnp.concatenate([one, one], axis=2)
+
+    serve(0)
+    arrive(own_up[0], own_down[1])
+    start(on_up, on_down)
+
     own = pl.ds(pl.multiple_of(me * 16, 16), 16)
     q_all[pl.ds(0, 16), pl.ds(0, 640)] = q_out[own, :]
     marks = (lax.broadcasted_iota(jnp.int32, (512, 128), 0) // 4) % 4 == lax.broadcasted_iota(
         jnp.int32, (512, 128), 1
     )
     q_all[:, 640:] = jnp.where(marks, 1.0, 0.0).astype(jnp.bfloat16)
-    for p in range(N):
-        owner = behind(me, OFFSETS[p])
-        for s in range(2):
-            wide = jnp.broadcast_to(bias[s, pl.ds(owner, 1), :], (QUARTER, 128)).astype(jnp.bfloat16)
-            for k in (2 * s, 2 * s + 1):
-                extra[k, p, :, pl.ds(128, 128)] = wide
+    for flip in (0, 1):
+        for e in range(4):
+            _, first_row, at = server(flip, e)
+            for w in range(4):
+                for i in (0, 1):
+                    mark = bias[i, pl.ds(first_row + (at + AXIS[w]) % 4, 1), :]
+                    extra[w, i, 4 * flip + e, :, pl.ds(128, 128)] = jnp.broadcast_to(mark, (BLK, 128)).astype(
+                        jnp.bfloat16
+                    )
+    arrive(own_up[1])
+    widen(1)
+
+    @pl.when((c == 1) & (y != 3))
+    def _():
+        arrive(down[:2])
+
+    @pl.when(c == 1)
+    def _():
+        start(over)
+
+    serve(1)
+    arrive(own_down[0])
+    widen(2)
+    serve(2)
     settled(q_all.at[pl.ds(16, 496), pl.ds(0, 640)], q_ss, q_rs).wait_recv()
 
     scale = math.log2(math.e) / math.sqrt(192)
-    first = lax.broadcasted_iota(jnp.int32, (QUARTER, 128), 1) < 64
-    none = jnp.zeros((QUARTER, 128), jnp.bfloat16)
-
-    def unpack(turns, put):
-        for b in range(2):
-            both = jnp.concatenate([turns[:, 256 * b + 128 * i : 256 * b + 128 * i + 128] for i in range(2)], axis=0)
-            put(b, jnp.where(first, both, none))
-            put(2 + b, jnp.where(first, none, both))
+    first = lax.broadcasted_iota(jnp.int32, (BLK, 128), 1) < 64
+    none = jnp.zeros((BLK, 128), jnp.bfloat16)
+
+    def unpack(turns):
+        both = jnp.concatenate([turns[:, 128 * b : 128 * b + 128] for b in range(4)], axis=0)
+        return jnp.where(first, both, none), jnp.where(first, none, both)
 
     def scores(latent, more):
         s = lax.dot_general(q_all[:, :DL], latent, lanes, preferred_element_type=jnp.float32)
@@ -262,28 +331,28 @@
     total[...] = jnp.zeros((512, 1), jnp.float32)
     acc[...] = jnp.zeros((512, DL), jnp.float32)
 
+    def attend(w):
+        settled(keys_turn.at[w, pl.ds(1, 7)], t_ss.at[w], t_rs.at[w]).wait_recv()
+        for j in range(8):
+            for i, values in enumerate(unpack(keys_turn[w, j])):
+                extra[w, i, j, :, pl.ds(0, 128)] = values
+        for i in (0, 1):
+            settled(keys.at[w, i, pl.ds(1, 7)], k_ss.at[w, i], k_rs.at[w, i]).wait_recv()
+            add(keys[w, i].reshape(512, DL), extra[w, i].reshape(512, 256))
+
+    attend(0)
+    arrive(on_up, on_down)
+    widen(3)
+    serve(3)
+
     @pl.when(c == 0)
     def _():
-        for copy in over:
-            copy.wait_recv()
-
-    hot_more = []
-    unpack(hot_turn[...], lambda k, values: hot_more.append((k, values)))
-    hot_more = jnp.concatenate([values for _, values in sorted(hot_more, key=lambda item: item[0])], axis=0)
+        arrive(over)
+
+    hot_more = jnp.concatenate(unpack(hot_turn[...]), axis=0)
     add(hot[...].reshape(128, DL), jnp.concatenate([hot_more, jnp.zeros_like(hot_more)], axis=1))
-
-    settled(keys_turn.at[pl.ds(1, N - 1)], t_ss, t_rs).wait_recv()
-    for p in range(N):
-
-        def put(k, values, p=p):
-            extra[k, p, :, pl.ds(0, 128)] = values
-
-        unpack(keys_turn[p], put)
-    for k in range(PARTS):
-        for j in range(2):
-            settled(keys.at[k, pl.ds(1, 15) if j == 0 else pl.ds(16, 16)], k_ss.at[k], k_rs.at[k, j]).wait_recv()
-            run = pl.ds(16 * j, 16)
-            add(keys[k, run].reshape(512, DL), extra[k, run].reshape(512, 256))
+    for w in (1, 2, 3):
+        attend(w)
 
     lat_out[...] = (acc[...] / total[...]).astype(jnp.bfloat16)
     for p in range(1, N):
@@ -302,11 +371,14 @@
         result = jnp.where(row % 4 == h, jnp.dot(got, absorb_v[h], preferred_element_type=jnp.float32), result)
     out[...] = result.astype(jnp.bfloat16)
 
-    settled(ids_in.at[pl.ds(1, N - 1)], ids_ss, ids_rs).wait_send()
+    settled(ids_in.at[pl.ds(1, 7)], ids_ss, ids_rs).wait_send()
     settled(q_out.at[pl.ds(0, 496)], q_ss, q_rs).wait_send()
-    settled(stage_turn.at[pl.ds(1, N - 1)], t_ss, t_rs).wait_send()
-    for k in range(PARTS):
-        settled(stage.at[k, pl.ds(1, N - 1)], k_ss.at[k], k_rs.at[k, 0]).wait_send()
+    for copy in own_up[0] + own_up[1] + own_down[0] + own_down[1] + on_up + on_down:
+        copy.wait_send()
+    for w in range(4):
+        settled(stage_turn.at[w, pl.ds(1, 7)], t_ss.at[w], t_rs.at[w]).wait_send()
+        for i in (0, 1):
+            settled(stage.at[w, i, pl.ds(1, 7)], k_ss.at[w, i], k_rs.at[w, i]).wait_send()
     settled(lat_out.at[pl.ds(0, 496)], o_ss, o_rs).wait_send()
 
     @pl.when(me == N - 1)
@@ -340,27 +412,32 @@
             pltpu.VMEM((4, DL, 128), bf16),
             pltpu.VMEM((576, 1024), bf16),
             pltpu.VMEM((16, BLK, DL), bf16),
-            pltpu.VMEM((16, BLK, 128), bf16),
+            pltpu.VMEM((16, BLK, DL), bf16),
+            pltpu.VMEM((16, BLK, DL), bf16),
+            pltpu.VMEM((16, BLK, DL), bf16),
+            pltpu.VMEM((4, 16, BLK, 128), bf16),
+            pltpu.VMEM((4, 8, BLK, 128), bf16),
             pltpu.VMEM((N, 1, 128), i32),
-            pltpu.VMEM((N, 1, 128), i32),
-            pltpu.SMEM((N, 1, 128), i32),
+            pltpu.VMEM((8, 4, 1, 128), i32),
+            pltpu.SMEM((8, 4, 1, 128), i32),
             pltpu.VMEM((2, N, 128), f32),
             pltpu.VMEM((512, 640), bf16),
             pltpu.VMEM((512, 768), bf16),
-            pltpu.VMEM((PARTS, N, QUARTER, DL), bf16),
-            pltpu.VMEM((N, 16, DL), bf16),
-            pltpu.VMEM((PARTS, N, QUARTER, DL), bf16),
-            pltpu.VMEM((N, 16, DL), bf16),
-            pltpu.VMEM((PARTS, QUARTER, DL), bf16),
+            pltpu.VMEM((4, 2, 8, BLK, DL), bf16),
+            pltpu.VMEM((4, 8, 16, DL), bf16),
+            pltpu.VMEM((4, 2, 8, BLK, DL), bf16),
+            pltpu.VMEM((4, 8, 16, DL), bf16),
+            pltpu.VMEM((2, BLK, DL), bf16),
             pltpu.VMEM((16, DL), bf16),
-            pltpu.VMEM((PARTS, N, QUARTER, 256), bf16),
+            pltpu.VMEM((4, 2, 8, BLK, 256), bf16),
             pltpu.VMEM((512, 1), f32),
             pltpu.VMEM((512, 1), f32),
             pltpu.VMEM((512, DL), f32),
             pltpu.VMEM((512, DL), bf16),
             pltpu.VMEM((512, DL), bf16),
         ]
-        + [dma, dma, dma, dma, dma((PARTS,)), dma((PARTS, 2)), dma, dma, dma, dma]
+        + [dma, dma, dma((2, 2, 2)), dma((2, 2, 2)), dma((2, 2)), dma((2, 2)), dma, dma]
+        + [dma((4, 2)), dma((4, 2)), dma((4,)), dma((4,)), dma, dma]
         + [dma((2, 7)), dma((2,)), dma, dma((4,))],
         compiler_params=pltpu.CompilerParams(collective_id=0, has_side_effects=True, vmem_limit_bytes=64 * 2**20 - 160 * 2**10),
     )(

time: 93.5 us -> 81 us (0.87)
  Pallas kernels: 91.7 us -> 79.2 us
    pallas_call x1, Pallas kernels: 91.7 us -> 79.2 us  [body(): pl.pallas_call(kernel, out_shape=jax.ShapeDtypeStruct((512, 128), bf16),...]
where the time goes in v3:
time: 81 us; the launch traced here: 80.8 us
  Pallas kernels  79.2 us (98%)
  local copies, waits for them, and re-layouts  1.61 us (2%)
    pallas_call x1, Pallas kernels, body(): pl.pallas_call(kernel, out_shape=jax.ShapeDtypeStruct((512, 128), bf16),...  79.2 us

profile of v3, /device:TPU:1, one launch (start us, length us, event | category | flops | bytes accessed | tf_op | source)
XLA Modules:
  0.0 80.8 jit_solution(7461119614141860936)
XLA Ops:
  0.0 79.2 %shard_map.55 = bf16[512,128]{1,0:T(8,128)(2,1)} custom-call(bf16[4,192,128]{2,1,0:T(8,128)(2,1)} %bitcast.7, bf16[512,512]{1,0:T(8,128)(2,1)} %bitcast.6, bf16[4,512,128]{2,1,0:T(8,128)(2,1)} %absorb_v_at.1, bf16[576,1024]{1,0:T(8,128)(2,1)} %bitcast.4, s32[4,30]{1,0:T(4,128)} %cold.1), custom_call_target="tpu_custom_call" | custom-call | tf_op jit(solution)/shard_map/pallas_call | solution.py:404
  79.2 1.6 %copy.7 = bf16[128,4,128]{2,1,0:T(4,128)(2,1)} copy(bf16[128,4,128]{2,1,0:T(4,128)(2,1)} %bitcast.5) | data formatting | bytes 262144

commit v4 on v3

--- a/solution.py
+++ b/solution.py
@@ -19,11 +19,11 @@
 SERVED = ((0, 1), (0, 3), (0, 2), (1, 1), (1, 3), (1, 2), (1, 0))
 
 RINGS = (
+    ((2, 2),),
+    ((2, 1), (1, 2), (2, 3), (3, 2)),
     ((1, 1), (3, 3), (1, 3), (3, 1)),
-    ((2, 1), (0, 1), (2, 3), (0, 3)),
-    ((2, 2),),
-    ((1, 2), (1, 0), (3, 2), (3, 0)),
     ((2, 0), (0, 2)),
+    ((1, 0), (0, 1), (3, 0), (0, 3)),
 )
 OFFSETS = [(0, 0, 0)]
 for ring in RINGS:
@@ -61,7 +61,7 @@
     query, absorb_k, absorb_v, stored,
     rows0, rows1, rows2, rows3, rope, pairs, ids_out, ids_in, ids, bias, q_out, q_all, stage, stage_turn, keys, keys_turn, hot, hot_turn, extra,
     top, total, acc, lat_out, lat_in,
-    ids_ss, ids_rs, own_ss, own_rs, fwd_ss, fwd_rs, q_ss, q_rs, k_ss, k_rs, t_ss, t_rs, o_ss, o_rs, hot_ss, hot_rs, id_sem, in_sem,
+    ids_ss, ids_rs, own_ss, own_rs, fwd_ss, fwd_rs, q_ss, q_rs, k_ss, k_rs, t_ss, t_rs, o_ss, o_rs, hot_ss, hot_rs, id_sem, in_sem, all_in,
 ):
     me = lax.axis_index("ctx")
     x, y, c = me // 8, (me // 2) % 4, me % 2
@@ -85,8 +85,9 @@
         return device(core, (cu + 4 - e) % 4, cv), core * 16 + (cu + 4 - e) % 4 * 4, cv
 
     barrier = pltpu.get_barrier_semaphore()
-    for p in range(1, N):
-        pl.semaphore_signal(barrier, inc=1, **to(ahead(me, OFFSETS[p])))
+    crossing = [offset for offset in OFFSETS[1:] if 0 in offset[:2]]
+    for offset in crossing:
+        pl.semaphore_signal(barrier, inc=1, **to(ahead(me, offset)))
 
     loads = [
         pltpu.make_async_copy(src, dst, in_sem.at[k])
@@ -138,7 +139,9 @@
     low_lanes = lax.broadcasted_iota(jnp.int32, (8, BLK, 128), 2) < 64
     pairs[0] = jnp.where(low_lanes, rope[0, pl.ds(0, 8)], rope[0, pl.ds(8, 8)])
 
-    pl.semaphore_wait(barrier, N - 1)
+    pl.semaphore_wait(barrier, len(crossing))
+    for offset in crossing:
+        pl.semaphore_signal(all_in, inc=1, **to(ahead(me, offset)))
     for flip, e in SERVED:
         there, first_row, _ = server(flip, e)
         pltpu.make_async_remote_copy(
@@ -212,6 +215,7 @@
     ).astype(jnp.bfloat16)
     turn = turn.astype(jnp.bfloat16)
     q_out[:, DL:] = jnp.concatenate([turn, turn], axis=1)
+    pl.semaphore_wait(all_in, len(crossing))
     for p in range(1, N):
         dst = ahead(me, OFFSETS[p])
         pltpu.make_async_remote_copy(
@@ -253,7 +257,7 @@
             j = 4 * flip + e
             pltpu.make_async_remote_copy(
                 src_ref=stage.at[w, 1, j], dst_ref=keys.at[w, 1, j],
-                send_sem=k_ss.at[w, 1], recv_sem=k_rs.at[w, 1], **to(served(flip, e))
+                send_sem=k_ss.at[w, 1], recv_sem=k_rs.at[w, 1 + flip], **to(served(flip, e))
             ).start()
         pack(
             rows[w], rope.at[w], ids[0, at, 0, 0], ids[0, at, 0, 1],
@@ -300,7 +304,6 @@
     arrive(own_down[0])
     widen(2)
     serve(2)
-    settled(q_all.at[pl.ds(16, 496), pl.ds(0, 640)], q_ss, q_rs).wait_recv()
 
     scale = math.log2(math.e) / math.sqrt(192)
     first = lax.broadcasted_iota(jnp.int32, (BLK, 128), 1) < 64
@@ -310,20 +313,17 @@
         both = jnp.concatenate([turns[:, 128 * b : 128 * b + 128] for b in range(4)], axis=0)
         return jnp.where(first, both, none), jnp.where(first, none, both)
 
-    def scores(latent, more):
-        s = lax.dot_general(q_all[:, :DL], latent, lanes, preferred_element_type=jnp.float32)
-        s += lax.dot_general(q_all[:, DL:], more, lanes, preferred_element_type=jnp.float32)
-        return s * scale
-
-    def add(latent, more):
-        s = scores(latent, more)
-        old = top[...]
+    def add(latent, more, part=slice(None)):
+        s = lax.dot_general(q_all[part, :DL], latent, lanes, preferred_element_type=jnp.float32)
+        s += lax.dot_general(q_all[part, DL:], more, lanes, preferred_element_type=jnp.float32)
+        s *= scale
+        old = top[part]
         new = jnp.maximum(old, jnp.max(s, axis=1, keepdims=True))
         fade = jnp.exp2(old - new)
         w = jnp.exp2(s - new)
-        total[...] = total[...] * fade + jnp.sum(w, axis=1, keepdims=True)
-        top[...] = new
-        acc[...] = acc[...] * fade + jnp.dot(
+        total[part] = total[part] * fade + jnp.sum(w, axis=1, keepdims=True)
+        top[part] = new
+        acc[part] = acc[part] * fade + jnp.dot(
             w.astype(jnp.bfloat16), latent, preferred_element_type=jnp.float32
         )
 
@@ -331,15 +331,26 @@
     total[...] = jnp.zeros((512, 1), jnp.float32)
     acc[...] = jnp.zeros((512, DL), jnp.float32)
 
-    def attend(w):
+    def prepare(w):
         settled(keys_turn.at[w, pl.ds(1, 7)], t_ss.at[w], t_rs.at[w]).wait_recv()
         for j in range(8):
             for i, values in enumerate(unpack(keys_turn[w, j])):
                 extra[w, i, j, :, pl.ds(0, 128)] = values
+
+    def landed(w, i, flips=(0, 1)):
+        for flip in flips if i else (0,):
+            span = pl.ds(4 * flip + 1 - flip, 3 + flip) if i else pl.ds(1, 7)
+            settled(keys.at[w, i, span], k_ss.at[w, i], k_rs.at[w, i + flip]).wait_recv()
+        run = pl.ds(4 * flips[0], 4 * len(flips))
+        tokens = 256 * len(flips)
+        return keys[w, i, run].reshape(tokens, DL), extra[w, i, run].reshape(tokens, 256)
+
+    def attend(w):
+        prepare(w)
         for i in (0, 1):
-            settled(keys.at[w, i, pl.ds(1, 7)], k_ss.at[w, i], k_rs.at[w, i]).wait_recv()
-            add(keys[w, i].reshape(512, DL), extra[w, i].reshape(512, 256))
-
+            add(*landed(w, i))
+
+    settled(q_all.at[pl.ds(16, 496), pl.ds(0, 640)], q_ss, q_rs).wait_recv()
     attend(0)
     arrive(on_up, on_down)
     widen(3)
@@ -351,17 +362,22 @@
 
     hot_more = jnp.concatenate(unpack(hot_turn[...]), axis=0)
     add(hot[...].reshape(128, DL), jnp.concatenate([hot_more, jnp.zeros_like(hot_more)], axis=1))
-    for w in (1, 2, 3):
-        attend(w)
-
-    lat_out[...] = (acc[...] / total[...]).astype(jnp.bfloat16)
-    for p in range(1, N):
-        dst = behind(me, OFFSETS[p])
-        pltpu.make_async_remote_copy(
-            src_ref=lat_out.at[pl.ds(16 * p, 16)],
-            dst_ref=lat_in.at[pl.ds(pl.multiple_of(me * 16, 16), 16)],
-            send_sem=o_ss, recv_sem=o_rs, **to(dst)
-        ).start()
+    attend(1)
+    attend(2)
+    prepare(3)
+    add(*landed(3, 0))
+    add(*landed(3, 1, (0,)))
+    last = landed(3, 1, (1,))
+    for half in (0, 1):
+        part = pl.ds(256 * half, 256)
+        add(*last, part)
+        lat_out[part] = (acc[part] * (1.0 / total[part])).astype(jnp.bfloat16)
+        for p in range(max(1, 16 * half), 16 * half + 16):
+            pltpu.make_async_remote_copy(
+                src_ref=lat_out.at[pl.ds(16 * p, 16)],
+                dst_ref=lat_in.at[pl.ds(pl.multiple_of(me * 16, 16), 16)],
+                send_sem=o_ss, recv_sem=o_rs, **to(behind(me, OFFSETS[p]))
+            ).start()
     lat_in[own, :] = lat_out[pl.ds(0, 16), :]
     settled(lat_in.at[pl.ds(0, 496)], o_ss, o_rs).wait_recv()
     loads[3].wait()
@@ -404,7 +420,7 @@
     out = pl.pallas_call(
         kernel,
         out_shape=jax.ShapeDtypeStruct((512, 128), bf16),
-        in_specs=[pl.BlockSpec(memory_space=pl.ANY)] * 4 + [vmem],
+        in_specs=[pl.BlockSpec(memory_space=pltpu.HBM)] * 4 + [vmem],
         out_specs=vmem,
         scratch_shapes=[
             pltpu.VMEM((4, 192, 128), bf16),
@@ -437,8 +453,8 @@
             pltpu.VMEM((512, DL), bf16),
         ]
         + [dma, dma, dma((2, 2, 2)), dma((2, 2, 2)), dma((2, 2)), dma((2, 2)), dma, dma]
-        + [dma((4, 2)), dma((4, 2)), dma((4,)), dma((4,)), dma, dma]
-        + [dma((2, 7)), dma((2,)), dma, dma((4,))],
+        + [dma((4, 2)), dma((4, 3)), dma((4,)), dma((4,)), dma, dma]
+        + [dma((2, 7)), dma((2,)), dma, dma((4,)), pltpu.SemaphoreType.REGULAR],
         compiler_params=pltpu.CompilerParams(collective_id=0, has_side_effects=True, vmem_limit_bytes=64 * 2**20 - 160 * 2**10),
     )(
         query.transpose(1, 2, 0),

time: 81 us -> 79.8 us (0.985)
  Pallas kernels: 79.2 us -> 78 us
    pallas_call x1, Pallas kernels: 79.2 us -> 78 us  [body(): pl.pallas_call(kernel, out_shape=jax.ShapeDtypeStruct((512, 128), bf16),...]
where the time goes in v4:
time: 79.8 us; the launch traced here: 79.6 us
  Pallas kernels  78 us (98%)
  local copies, waits for them, and re-layouts  1.61 us (2%)
    pallas_call x1, Pallas kernels, body(): pl.pallas_call(kernel, out_shape=jax.ShapeDtypeStruct((512, 128), bf16),...  78 us
    unnamed x1, local copies, waits for them, and re-layouts  1.61 us

profile of v4, /device:TPU:1, one launch (start us, length us, event | category | flops | bytes accessed | tf_op | source)
XLA Modules:
  0.0 79.6 jit_solution(6404781649278332491)
XLA Ops:
  0.0 78.0 %shard_map.55 = bf16[512,128]{1,0:T(8,128)(2,1)} custom-call(bf16[4,192,128]{2,1,0:T(8,128)(2,1)} %bitcast.7, bf16[512,512]{1,0:T(8,128)(2,1)} %bitcast.6, bf16[4,512,128]{2,1,0:T(8,128)(2,1)} %absorb_v_at.1, bf16[576,1024]{1,0:T(8,128)(2,1)} %bitcast.4, s32[4,30]{1,0:T(4,128)} %cold.1), custom_call_target="tpu_custom_call" | custom-call | tf_op jit(solution)/shard_map/pallas_call | solution.py:420
  78.0 1.6 %copy.7 = bf16[128,4,128]{2,1,0:T(4,128)(2,1)} copy(bf16[128,4,128]{2,1,0:T(4,128)(2,1)} %bitcast.5) | data formatting | bytes 262144

commit v5 on v4

--- a/solution.py
+++ b/solution.py
@@ -16,7 +16,7 @@
 NEG = -1e30
 
 AXIS = (0, 3, 1, 2)
-SERVED = ((0, 1), (0, 3), (0, 2), (1, 1), (1, 3), (1, 2), (1, 0))
+SERVED = ((0, 2), (0, 1), (0, 3), (1, 2), (1, 1), (1, 3), (1, 0))
 
 RINGS = (
     ((2, 2),),
@@ -57,10 +57,10 @@
 
 
 def kernel(
-    query_at, absorb_k_at, absorb_v_at, stored_at, cold, out,
-    query, absorb_k, absorb_v, stored,
+    query_at, absorb_k_at, absorb_v_at, stored_at, cold_at, out,
+    query, absorb_k, absorb_v, stored, cold,
     rows0, rows1, rows2, rows3, rope, pairs, ids_out, ids_in, ids, bias, q_out, q_all, stage, stage_turn, keys, keys_turn, hot, hot_turn, extra,
-    top, total, acc, lat_out, lat_in,
+    top, total, acc, lat_out, lat_in, values,
     ids_ss, ids_rs, own_ss, own_rs, fwd_ss, fwd_rs, q_ss, q_rs, k_ss, k_rs, t_ss, t_rs, o_ss, o_rs, hot_ss, hot_rs, id_sem, in_sem, all_in,
 ):
     me = lax.axis_index("ctx")
@@ -92,12 +92,16 @@
     loads = [
         pltpu.make_async_copy(src, dst, in_sem.at[k])
         for k, (src, dst) in enumerate(
-            ((stored_at, stored), (query_at, query), (absorb_k_at, absorb_k), (absorb_v_at, absorb_v))
+            (
+                (stored_at, stored), (query_at, query), (absorb_k_at, absorb_k), (absorb_v_at, absorb_v),
+                (cold_at, cold),
+            )
         )
     ]
     for load in loads:
         load.start()
 
+    loads[4].wait()
     line = lax.broadcasted_iota(jnp.int32, (N, 1), 0)
     core, cu, cv = line // 16, (line // 4) % 4, line % 4
     base = jnp.where(core == 0, cv * 8 + cu * 2, cu * 8 + cv * 2 + 1) * 16
@@ -334,8 +338,8 @@
     def prepare(w):
         settled(keys_turn.at[w, pl.ds(1, 7)], t_ss.at[w], t_rs.at[w]).wait_recv()
         for j in range(8):
-            for i, values in enumerate(unpack(keys_turn[w, j])):
-                extra[w, i, j, :, pl.ds(0, 128)] = values
+            for i, turned in enumerate(unpack(keys_turn[w, j])):
+                extra[w, i, j, :, pl.ds(0, 128)] = turned
 
     def landed(w, i, flips=(0, 1)):
         for flip in flips if i else (0,):
@@ -362,6 +366,9 @@
 
     hot_more = jnp.concatenate(unpack(hot_turn[...]), axis=0)
     add(hot[...].reshape(128, DL), jnp.concatenate([hot_more, jnp.zeros_like(hot_more)], axis=1))
+    loads[3].wait()
+    for h in range(4):
+        values[:, pl.ds(128 * h, 128)] = absorb_v[h]
     attend(1)
     attend(2)
     prepare(3)
@@ -380,11 +387,11 @@
             ).start()
     lat_in[own, :] = lat_out[pl.ds(0, 16), :]
     settled(lat_in.at[pl.ds(0, 496)], o_ss, o_rs).wait_recv()
-    loads[3].wait()
     got = lat_in[...]
-    result = jnp.zeros((512, 128), jnp.float32)
-    for h in range(4):
-        result = jnp.where(row % 4 == h, jnp.dot(got, absorb_v[h], preferred_element_type=jnp.float32), result)
+    wide = jnp.dot(got, values[...], preferred_element_type=jnp.float32)
+    result = wide[:, :128]
+    for h in range(1, 4):
+        result = jnp.where(row % 4 == h, wide[:, 128 * h : 128 * h + 128], result)
     out[...] = result.astype(jnp.bfloat16)
 
     settled(ids_in.at[pl.ds(1, 7)], ids_ss, ids_rs).wait_send()
@@ -420,13 +427,14 @@
     out = pl.pallas_call(
         kernel,
         out_shape=jax.ShapeDtypeStruct((512, 128), bf16),
-        in_specs=[pl.BlockSpec(memory_space=pltpu.HBM)] * 4 + [vmem],
+        in_specs=[pl.BlockSpec(memory_space=pltpu.HBM)] * 5,
         out_specs=vmem,
         scratch_shapes=[
             pltpu.VMEM((4, 192, 128), bf16),
             pltpu.VMEM((512, DL), bf16),
             pltpu.VMEM((4, DL, 128), bf16),
             pltpu.VMEM((576, 1024), bf16),
+            pltpu.VMEM((4, 30), i32),
             pltpu.VMEM((16, BLK, DL), bf16),
             pltpu.VMEM((16, BLK, DL), bf16),
             pltpu.VMEM((16, BLK, DL), bf16),
@@ -451,10 +459,11 @@
             pltpu.VMEM((512, DL), f32),
             pltpu.VMEM((512, DL), bf16),
             pltpu.VMEM((512, DL), bf16),
+            pltpu.VMEM((DL, 512), bf16),
         ]
         + [dma, dma, dma((2, 2, 2)), dma((2, 2, 2)), dma((2, 2)), dma((2, 2)), dma, dma]
         + [dma((4, 2)), dma((4, 3)), dma((4,)), dma((4,)), dma, dma]
-        + [dma((2, 7)), dma((2,)), dma, dma((4,)), pltpu.SemaphoreType.REGULAR],
+        + [dma((2, 7)), dma((2,)), dma, dma((5,)), pltpu.SemaphoreType.REGULAR],
         compiler_params=pltpu.CompilerParams(collective_id=0, has_side_effects=True, vmem_limit_bytes=64 * 2**20 - 160 * 2**10),
     )(
         query.transpose(1, 2, 0),

time: 79.8 us -> 78.5 us (0.984)
  Pallas kernels: 78 us -> 76.7 us
    pallas_call x1, Pallas kernels: 78 us -> 76.7 us  [body(): pl.pallas_call(kernel, out_shape=jax.ShapeDtypeStruct((512, 128), bf16),...]
where the time goes in v5:
time: 78.5 us; the launch traced here: 78.4 us
  Pallas kernels  76.7 us (98%)
  local copies, waits for them, and re-layouts  1.61 us (2%)
    pallas_call x1, Pallas kernels, body(): pl.pallas_call(kernel, out_shape=jax.ShapeDtypeStruct((512, 128), bf16),...  76.7 us
    unnamed x1, local copies, waits for them, and re-layouts  1.61 us

profile of v5, /device:TPU:1, one launch (start us, length us, event | category | flops | bytes accessed | tf_op | source)
XLA Modules:
  0.0 78.4 jit_solution(7914146760844480940)
XLA Ops:
  0.0 76.7 %shard_map.55 = bf16[512,128]{1,0:T(8,128)(2,1)} custom-call(bf16[4,192,128]{2,1,0:T(8,128)(2,1)} %bitcast.7, bf16[512,512]{1,0:T(8,128)(2,1)} %bitcast.6, bf16[4,512,128]{2,1,0:T(8,128)(2,1)} %absorb_v_at.1, bf16[576,1024]{1,0:T(8,128)(2,1)} %bitcast.4, s32[4,30]{1,0:T(4,128)} %cold_at.1), custom_call_target="tpu_custom_call" | custom-call | tf_op jit(solution)/shard_map/pallas_call | solution.py:427
  76.8 1.6 %copy.7 = bf16[128,4,128]{2,1,0:T(4,128)(2,1)} copy(bf16[128,4,128]{2,1,0:T(4,128)(2,1)} %bitcast.5) | data formatting | bytes 262144

commit v6 on v5

--- a/solution.py
+++ b/solution.py
@@ -92,16 +92,14 @@
     loads = [
         pltpu.make_async_copy(src, dst, in_sem.at[k])
         for k, (src, dst) in enumerate(
-            (
-                (stored_at, stored), (query_at, query), (absorb_k_at, absorb_k), (absorb_v_at, absorb_v),
-                (cold_at, cold),
-            )
+            [(stored_at.at[:, pl.ds(256 * n, 256)], stored.at[:, pl.ds(256 * n, 256)]) for n in range(4)]
+            + [(query_at, query), (absorb_k_at, absorb_k), (absorb_v_at, absorb_v), (cold_at, cold)]
         )
     ]
-    for load in loads:
+    for load in loads[7:] + loads[:7]:
         load.start()
 
-    loads[4].wait()
+    loads[7].wait()
     line = lax.broadcasted_iota(jnp.int32, (N, 1), 0)
     core, cu, cv = line // 16, (line // 4) % 4, line % 4
     base = jnp.where(core == 0, cv * 8 + cu * 2, cu * 8 + cv * 2 + 1) * 16
@@ -130,8 +128,8 @@
     unit = jnp.where(
         lax.broadcasted_iota(jnp.int32, (256, 256), 0) == lax.broadcasted_iota(jnp.int32, (256, 256), 1), 1.0, 0.0
     ).astype(jnp.bfloat16)
-    loads[0].wait()
     for k in range(4):
+        loads[k].wait()
         part = pl.ds(256 * k, 256)
         turned = lax.dot_general(unit, stored[:DL, part], lanes, preferred_element_type=jnp.float32)
         rows[0][pl.ds(4 * k, 4)] = turned.astype(jnp.bfloat16).reshape(4, BLK, DL)
@@ -207,8 +205,8 @@
     row = lax.broadcasted_iota(jnp.int32, (512, 128), 0)
     column = lax.broadcasted_iota(jnp.int32, (512, 128), 1)
     plain, turn = [], None
-    loads[1].wait()
-    loads[2].wait()
+    loads[4].wait()
+    loads[5].wait()
     for h in range(4):
         pick = jnp.where(row == 4 * column + h, 1.0, 0.0).astype(jnp.bfloat16)
         spread = lax.dot_general(pick, query[h], lanes, preferred_element_type=jnp.float32)
@@ -366,7 +364,7 @@
 
     hot_more = jnp.concatenate(unpack(hot_turn[...]), axis=0)
     add(hot[...].reshape(128, DL), jnp.concatenate([hot_more, jnp.zeros_like(hot_more)], axis=1))
-    loads[3].wait()
+    loads[6].wait()
     for h in range(4):
         values[:, pl.ds(128 * h, 128)] = absorb_v[h]
     attend(1)
@@ -463,7 +461,7 @@
         ]
         + [dma, dma, dma((2, 2, 2)), dma((2, 2, 2)), dma((2, 2)), dma((2, 2)), dma, dma]
         + [dma((4, 2)), dma((4, 3)), dma((4,)), dma((4,)), dma, dma]
-        + [dma((2, 7)), dma((2,)), dma, dma((5,)), pltpu.SemaphoreType.REGULAR],
+        + [dma((2, 7)), dma((2,)), dma, dma((8,)), pltpu.SemaphoreType.REGULAR],
         compiler_params=pltpu.CompilerParams(collective_id=0, has_side_effects=True, vmem_limit_bytes=64 * 2**20 - 160 * 2**10),
     )(
         query.transpose(1, 2, 0),

time: 78.5 us -> 78.5 us (level)
  no operation moved by 1% of the time
where the time goes in v6:
time: 78.5 us; the launch traced here: 78.4 us
  Pallas kernels  76.8 us (98%)
  local copies, waits for them, and re-layouts  1.61 us (2%)
    pallas_call x1, Pallas kernels, body(): pl.pallas_call(kernel, out_shape=jax.ShapeDtypeStruct((512, 128), bf16),...  76.8 us
    unnamed x1, local copies, waits for them, and re-layouts  1.61 us

profile of v6, /device:TPU:1, one launch (start us, length us, event | category | flops | bytes accessed | tf_op | source)
XLA Modules:
  0.0 78.4 jit_solution(14189149076661108943)
XLA Ops:
  0.0 76.8 %shard_map.55 = bf16[512,128]{1,0:T(8,128)(2,1)} custom-call(bf16[4,192,128]{2,1,0:T(8,128)(2,1)} %bitcast.7, bf16[512,512]{1,0:T(8,128)(2,1)} %bitcast.6, bf16[4,512,128]{2,1,0:T(8,128)(2,1)} %absorb_v_at.1, bf16[576,1024]{1,0:T(8,128)(2,1)} %bitcast.4, s32[4,30]{1,0:T(4,128)} %cold_at.1), custom_call_target="tpu_custom_call" | custom-call | tf_op jit(solution)/shard_map/pallas_call | solution.py:425
  76.8 1.6 %copy.7 = bf16[128,4,128]{2,1,0:T(4,128)(2,1)} copy(bf16[128,4,128]{2,1,0:T(4,128)(2,1)} %bitcast.5) | data formatting | bytes 262144
